TPU v7x, 512 devices: a whole 4x4x16 slice. The times are simulated.
512 devices in a mesh: row: 16 (over z), col: 32 (over y, x, core).
Axes of the slice: x: 4, y: 4, z: 16, core: 2. Of those that a mesh axis runs over, the one named last changes fastest.
Arguments:
- tokens: bfloat16 [2048, 8192], P('col', 'row'), may hold values from -6 to 6
- cotangent: bfloat16 [2048, 8192], P('col', 'row'), may hold values from -42.33202 to 42.33202
- gate_pre: bfloat16 [2048, 14336], P('row', 'col'), may hold values from -6 to 6
- up_act: bfloat16 [2048, 14336], P('row', 'col'), may hold values from -6 to 6
- gate_weight: bfloat16 [8192, 14336], P('row', 'col'), may hold values from -6 to 6
- up_weight: bfloat16 [8192, 14336], P('row', 'col'), may hold values from -6 to 6
- down_weight: bfloat16 [14336, 8192], P('col', 'row'), may hold values from -9 to 9
- moment_m: bfloat16 [14336, 8192], P('col', 'row'), may hold values from -6 to 6
- moment_v: bfloat16 [14336, 8192], P('col', 'row'), may hold values from 0.1 to 1.6015625
Outputs:
- grad_input: bfloat16 [2048, 8192], P('col', 'row')
- grad_gate: bfloat16 [8192, 14336], P('row', 'col')
- grad_up: bfloat16 [8192, 14336], P('row', 'col')
- new_m: bfloat16 [14336, 8192], P('col', 'row')
- new_v: bfloat16 [14336, 8192], P('col', 'row')
- step_down: bfloat16 [14336, 8192], P('col', 'row')
- trust_ratio: float32 [], replicated
All inputs are finite; a program needn't handle non-finite values.
Results may differ from a plain program's by a relative error of at most 0.03.
Values may be sent and summed in bfloat16 or wider, within the bound.
No kernel may reach another device: no remote copies, remote signals or barrier semaphores. Data moves between devices by JAX's collectives and lax.ppermute only.
A program may use at most 64 MiB of HBM per device.

v0:
```python
import functools

import jax
import jax.numpy as jnp
from jax import lax
from jax.experimental import pallas as pl
from jax.experimental.pallas import tpu as pltpu
from jax.sharding import PartitionSpec as P

D = 8192
FF = 14336
Z = 16
SIDE = 4
CHIPS = 16
COLS = 32
SCALE_WIDTH = float(D) ** (-0.5)
SCALE_HIDDEN = float(FF) ** (-0.5)
BF16 = jnp.bfloat16
F32 = jnp.float32
VMEM = pl.BlockSpec(memory_space=pltpu.VMEM)
SMEM = pl.BlockSpec(memory_space=pltpu.SMEM)


def params():
    return pltpu.CompilerParams(vmem_limit_bytes=20 * 1024 * 1024)


def shift_z(v, step):
    pairs = []
    for z in range(Z):
        for col in range(COLS):
            way = step if col % 2 == 0 else -step
            pairs.append((z * COLS + col, (z + way) % Z * COLS + col))
    return lax.ppermute(v, ("row", "col"), pairs)


def swap_core(v):
    return lax.ppermute(v, "col", [(c, c ^ 1) for c in range(COLS)])


def exchange_chips(v):
    groups = [[2 * chip + core for chip in range(CHIPS)] for core in range(2)]
    return lax.all_to_all(v, "col", 0, 0, axis_index_groups=groups, tiled=True)


def gather_chips(v):
    mine = exchange_chips(jnp.broadcast_to(v[None], (CHIPS, *v.shape)))
    return mine, swap_core(mine)


def add(*terms):
    total = terms[0].astype(F32)
    for term in terms[1:]:
        total = total + term.astype(F32)
    return total.astype(BF16)


def reduce_z(zero, far, odd, even, give_odd, give_even, extra):
    own = shift_z(odd, 1)
    got_odd = swap_core(give_odd)
    their = shift_z(got_odd, 1)
    far = shift_z(far, SIDE)
    got_even = swap_core(give_even)
    moving_their = add(got_even[2], their[3])
    moving = add(even[2], own[3])
    for k in (2, 1):
        moving_their = shift_z(moving_their, 2)
        moving = shift_z(moving, 2)
        if k == 1:
            moving_their, moving, extra = lax.optimization_barrier((moving_their, moving, extra))
        moving_their = add(moving_their, got_even[k - 1], their[k])
        moving = add(moving, even[k - 1], own[k], *([far] if k == 2 else []))
    moving_their = shift_z(moving_their, 2)
    moving = shift_z(moving, 2)
    other = jnp.concatenate([add(moving_their, their[0]), jnp.zeros_like(extra)], axis=0)
    mine = jnp.concatenate([add(zero, moving, own[0]), extra], axis=0)
    got_mine = swap_core(other)
    got_other = swap_core(mine)
    return add(mine, got_mine), add(other, got_other)


GROUPS = ((0, -2, -4, -6), (2, 4, 6), (-1, -3, -5, -7), (1, 3, 5, 7, -8))


def owner_of(place_ref, offset):
    z, way = place_ref[0], place_ref[2]
    return lax.rem(z + way * offset + Z, Z)


def hidden_partial_body(place_ref, mine_ref, other_ref, weight_ref, cot_ref, *refs):
    zero_ref, far_ref, odd_ref, even_ref, give_odd_ref, give_even_ref, hold = refs
    core = place_ref[1]
    chips, rows, _ = mine_ref.shape
    for chip in range(chips):
        own = pl.multiple_of(chip * 2 * rows + core * rows, rows)
        their = pl.multiple_of(chip * 2 * rows + (1 - core) * rows, rows)
        cot_ref[pl.ds(own, rows), :] = mine_ref[chip]
        cot_ref[pl.ds(their, rows), :] = other_ref[chip]
    tokens = cot_ref.shape[0]
    width = tokens // Z
    span = tokens // SIDE
    for part in range(SIDE):
        product = lax.dot_general(
            weight_ref[...],
            cot_ref[part * span : (part + 1) * span, :],
            (((1,), (1,)), ((), ())),
            preferred_element_type=F32,
        )
        hold[:, part * span : (part + 1) * span] = (product * SCALE_HIDDEN).astype(BF16)

    def block(offset):
        start = pl.multiple_of(owner_of(place_ref, offset) * width, width)
        return hold[:, pl.ds(start, width)]

    zero_ref[...] = block(0)
    far_ref[...] = block(8)
    for k, offset in enumerate((1, 3, 5, 7)):
        odd_ref[k] = block(offset)
        give_odd_ref[k] = block(-offset)
    for k, offset in enumerate((2, 4, 6)):
        even_ref[k] = block(offset)
        give_even_ref[k] = block(-offset)


def hidden_partial(place, mine, other, weight):
    units, depth = weight.shape
    tokens = mine.shape[0] * mine.shape[1] * 2
    width = tokens // Z
    shapes = [(tokens, depth), (units, width), (units, width)]
    shapes += [(count, units, width) for count in (4, 3, 4, 3)]
    return pl.pallas_call(
        hidden_partial_body,
        out_shape=[jax.ShapeDtypeStruct(shape, BF16) for shape in shapes],
        in_specs=[SMEM] + [VMEM] * 3,
        out_specs=[VMEM] * 7,
        scratch_shapes=[pltpu.VMEM((units, tokens), BF16)],
        compiler_params=params(),
        cost_estimate=pl.CostEstimate(
            flops=2 * units * depth * tokens,
            bytes_accessed=2 * (2 * tokens * depth + units * depth + units * tokens),
            transcendentals=0,
        ),
        name="hidden_partial",
    )(place, mine, other, weight)


def down_body(acts_ref, cot_ref, weight_ref, m_ref, v_ref, *refs):
    swish_ref, slope_ref, new_m_ref, new_v_ref, update_ref, sums_ref = refs[:6]
    hidden, product = refs[6:]
    blocks, units, width = acts_ref.shape
    units = units // 2
    chunk = 64
    for k in range(blocks):
        cols = slice(k * width, (k + 1) * width)

        @pl.loop(0, units // chunk)
        def _(i, k=k, cols=cols):
            low = pl.multiple_of(i * chunk, chunk)
            rows = pl.ds(low, chunk)
            g = acts_ref[k, rows, :].astype(F32)
            u = acts_ref[k, pl.ds(low + units, chunk), :].astype(F32)
            s = jax.nn.sigmoid(g)
            swish = g * s
            slope = u * s * (1.0 + g * (1.0 - s))
            hidden[rows, cols] = (swish * u).astype(BF16)
            swish_ref[rows, cols] = swish.astype(BF16)
            slope_ref[rows, cols] = slope.astype(BF16)

    product[...] = lax.dot_general(
        hidden[...], cot_ref[...], (((1,), (0,)), ((), ())), preferred_element_type=F32
    )
    step = 16
    depth = product.shape[1]

    def optimizer(i, carry):
        weight_sum, update_sum = carry
        rows = pl.ds(pl.multiple_of(i * step, step), step)
        grad = product[rows, :] * SCALE_HIDDEN
        weight = weight_ref[rows, :].astype(F32)
        first = 0.9 * m_ref[rows, :].astype(F32) + 0.1 * grad
        second = 0.95 * v_ref[rows, :].astype(F32) + 0.05 * grad * grad
        update = first / (jnp.sqrt(second) + 1e-08) + 0.1 * weight
        new_m_ref[rows, :] = first.astype(BF16)
        new_v_ref[rows, :] = second.astype(BF16)
        update_ref[rows, :] = update
        return weight_sum + weight * weight, update_sum + update * update

    zero = jnp.zeros((step, depth), F32)
    weight_sum, update_sum = lax.fori_loop(0, units // step, optimizer, (zero, zero))
    weight_sum = jnp.sum(weight_sum, axis=0, keepdims=True)
    update_sum = jnp.sum(update_sum, axis=0, keepdims=True)
    lanes = sums_ref.shape[1]
    parts = [slice(k, k + lanes) for k in range(0, depth, lanes)]
    weight_sum = sum(weight_sum[:, part] for part in parts)
    update_sum = sum(update_sum[:, part] for part in parts)
    sums_ref[...] = in_rows(weight_sum, update_sum)


def in_rows(first, second):
    row = lax.broadcasted_iota(jnp.int32, (16, first.shape[1]), 0)
    value = jnp.where((row & 1) == 0, first, second)
    high = value.astype(BF16).astype(F32)
    middle = (value - high).astype(BF16).astype(F32)
    low = value - high - middle
    rest = jnp.where(row < 4, middle, jnp.where(row < 6, low, 0.0))
    return jnp.where(row < 2, high, rest).astype(BF16)


def from_rows(rows):
    first = rows[0:1] + rows[2:3] + rows[4:5]
    second = rows[1:2] + rows[3:4] + rows[5:6]
    return jnp.sum(first, axis=1, keepdims=True), jnp.sum(second, axis=1, keepdims=True)


def down_update(acts, cotangent, weight, moment_m, moment_v):
    units = acts.shape[1] // 2
    tokens, depth = cotangent.shape
    shapes = [
        jax.ShapeDtypeStruct((units, tokens), BF16),
        jax.ShapeDtypeStruct((units, tokens), BF16),
        jax.ShapeDtypeStruct((units, depth), BF16),
        jax.ShapeDtypeStruct((units, depth), BF16),
        jax.ShapeDtypeStruct((units, depth), F32),
        jax.ShapeDtypeStruct((16, 128), BF16),
    ]
    return pl.pallas_call(
        down_body,
        out_shape=shapes,
        in_specs=[VMEM] * 5,
        out_specs=[VMEM] * 6,
        scratch_shapes=[pltpu.VMEM((units, tokens), BF16), pltpu.VMEM((units, depth), F32)],
        compiler_params=params(),
        cost_estimate=pl.CostEstimate(
            flops=2 * units * depth * tokens + 30 * units * tokens,
            bytes_accessed=8 * units * tokens + 2 * tokens * depth + 14 * units * depth,
            transcendentals=units * tokens,
        ),
        name="down_update",
    )(acts, cotangent, weight, moment_m, moment_v)


def group_body(number, count, place_ref, *refs):
    grads = refs[:count]
    swish_ref, slope_ref, gate_weight_ref, up_weight_ref = refs[count : count + 4]
    befores = refs[count + 4 : -6]
    gateact_ref, upact_ref, mine_ref, other_ref, sums_ref, hold = refs[-6:]
    units = gateact_ref.shape[0]
    blocks, half, _ = mine_ref.shape
    width = 2 * half
    chunk = 64
    core = place_ref[1]

    def block(k, rows):
        if k == 4:
            return grads[1][rows, :].astype(F32)
        return grads[0][k, rows, :].astype(F32)

    sums = befores[0][...] if befores else 0.0
    for k in range(blocks):
        sums = sums + block(k, slice(units, units + 16))
    sums_ref[...] = sums
    for k, offset in enumerate(GROUPS[number]):
        start = pl.multiple_of(owner_of(place_ref, offset) * width, width)
        cols = slice(k * width, (k + 1) * width)

        @pl.loop(0, units // chunk)
        def _(i, k=k, start=start, cols=cols):
            rows = pl.ds(pl.multiple_of(i * chunk, chunk), chunk)
            grad = block(k, rows)
            swish = swish_ref[rows, pl.ds(start, width)].astype(F32)
            slope = slope_ref[rows, pl.ds(start, width)].astype(F32)
            upact_ref[rows, cols] = (grad * swish).astype(BF16)
            gateact_ref[rows, cols] = (grad * slope).astype(BF16)

    contract_first = (((0,), (0,)), ((), ()))
    product = lax.dot_general(
        gateact_ref[...], gate_weight_ref[...], contract_first, preferred_element_type=F32
    )
    product = product + lax.dot_general(
        upact_ref[...], up_weight_ref[...], contract_first, preferred_element_type=F32
    )
    hold[...] = (product * SCALE_WIDTH).astype(BF16)
    for k in range(blocks):
        own = pl.multiple_of(k * width + core * half, half)
        their = pl.multiple_of(k * width + (1 - core) * half, half)
        mine_ref[k] = hold[pl.ds(own, half), :]
        low = other_ref.shape[0] - (blocks - k) * half - (16 if number == 3 else 0)
        other_ref[low : low + half, :] = hold[pl.ds(their, half), :]
    if number == 3:
        other_ref[blocks * half :, :] = jnp.zeros((16, other_ref.shape[1]), BF16)
        first = sums[0:1] + sums[2:3] + sums[4:5]
        second = sums[1:2] + sums[3:4] + sums[5:6]
        other_ref[blocks * half :, 0:128] = in_rows(first, second)
    elif number > 0:
        earlier = befores[1].shape[0]
        other_ref[0:earlier, :] = befores[1][...]


def input_group(number, place, grads, swish, slope, gate_weight, up_weight, *befores):
    units, tokens = swish.shape
    depth = gate_weight.shape[1]
    width = tokens // Z
    blocks = len(GROUPS[number])
    half = jax.ShapeDtypeStruct((blocks, width // 2, depth), BF16)
    if number == 3:
        other_rows = blocks * width // 2 + 16
    else:
        other_rows = sum(len(offsets) for offsets in GROUPS[: number + 1]) * width // 2
    other = jax.ShapeDtypeStruct((other_rows, depth), BF16)
    acts = jax.ShapeDtypeStruct((units, blocks * width), BF16)
    sums = jax.ShapeDtypeStruct((16, 128), F32)
    return pl.pallas_call(
        functools.partial(group_body, number, len(grads)),
        out_shape=[acts, acts, half, other, sums],
        in_specs=[SMEM] + [VMEM] * (4 + len(grads) + len(befores)),
        out_specs=[VMEM] * 5,
        scratch_shapes=[pltpu.VMEM((blocks * width, depth), BF16)],
        compiler_params=params(),
        cost_estimate=pl.CostEstimate(
            flops=4 * units * depth * blocks * width,
            bytes_accessed=10 * units * blocks * width + 4 * units * depth,
            transcendentals=0,
        ),
        name="input_group",
    )(place, *grads, swish, slope, gate_weight, up_weight, *befores)


def merge_body(place_ref, *refs):
    mine = refs[:SIDE]
    first_other_ref, last_other_ref, sums_ref, out_ref = refs[SIDE:]
    rows, depth = mine[0].shape[1:]
    parts = [(q * rows, slice(q * 128, (q + 1) * 128)) for q in range(depth // 128)]
    for number, offsets in enumerate(GROUPS):
        for k, offset in enumerate(offsets):
            chip = owner_of(place_ref, offset)
            for low, cols in parts:
                out_ref[chip, low : low + rows, :] = mine[number][k, :, cols]
    first = [offset for offsets in GROUPS[:3] for offset in offsets]
    for ref, offsets in ((first_other_ref, first), (last_other_ref, GROUPS[3])):
        for k, offset in enumerate(offsets):
            chip = owner_of(place_ref, -offset)
            for low, cols in parts:
                total = out_ref[chip, low : low + rows, :].astype(F32)
                total = total + ref[k * rows : (k + 1) * rows, cols].astype(F32)
                out_ref[chip, low : low + rows, :] = total.astype(BF16)
    their = last_other_ref[len(GROUPS[3]) * rows :, 0:128].astype(F32)
    first, second = from_rows(sums_ref[...] + their)
    sums = in_rows(jnp.broadcast_to(first, (1, 128)), jnp.broadcast_to(second, (1, 128)))
    for chip in range(out_ref.shape[0]):
        out_ref[chip, len(parts) * rows :, :] = sums


def merge_cores(place, mine, first_other, last_other, sums):
    _, rows, depth = mine[0].shape
    return pl.pallas_call(
        merge_body,
        out_shape=jax.ShapeDtypeStruct((CHIPS, rows * depth // 128 + 16, 128), BF16),
        in_specs=[SMEM] + [VMEM] * (SIDE + 3),
        out_specs=VMEM,
        compiler_params=params(),
        cost_estimate=pl.CostEstimate(
            flops=CHIPS * rows * depth, bytes_accessed=6 * CHIPS * rows * depth, transcendentals=0
        ),
        name="merge_cores",
    )(place, *mine, first_other, last_other, sums)


def finish_body(arrived_ref, update_ref, grad_input_ref, step_ref, ratio_ref):
    chips = arrived_ref.shape[0]
    rows, depth = grad_input_ref.shape
    for q in range(depth // 128):
        for low in range(0, rows, 32):
            part = slice(q * rows + low, q * rows + low + 32)
            total = arrived_ref[0, part, :].astype(F32)
            for chip in range(1, chips):
                total = total + arrived_ref[chip, part, :].astype(F32)
            grad_input_ref[low : low + 32, q * 128 : (q + 1) * 128] = total.astype(BF16)
    part = slice(rows * depth // 128, rows * depth // 128 + 16)
    sums = arrived_ref[0, part, :].astype(F32)
    for chip in range(1, chips):
        sums = sums + arrived_ref[chip, part, :].astype(F32)
    weight_total = sums[0:1] + sums[2:3] + sums[4:5]
    update_total = sums[1:2] + sums[3:4] + sums[5:6]
    ratio = jnp.sqrt(weight_total) / jnp.sqrt(update_total + 1e-06)
    ratio_ref[...] = ratio
    ratio = ratio[:, 0:1]
    step = 16

    @pl.loop(0, update_ref.shape[0] // step)
    def _(i):
        part = pl.ds(pl.multiple_of(i * step, step), step)
        step_ref[part, :] = (ratio * update_ref[part, :]).astype(BF16)


def finish(arrived, update):
    chips, rows, _ = arrived.shape
    units, depth = update.shape
    return pl.pallas_call(
        finish_body,
        out_shape=[
            jax.ShapeDtypeStruct(((rows - 16) * 128 // depth, depth), BF16),
            jax.ShapeDtypeStruct((units, depth), BF16),
            jax.ShapeDtypeStruct((1, 128), F32),
        ],
        in_specs=[VMEM] * 2,
        out_specs=[VMEM] * 3,
        compiler_params=params(),
        cost_estimate=pl.CostEstimate(
            flops=chips * rows * 128,
            bytes_accessed=2 * chips * rows * 128 + 6 * units * depth,
            transcendentals=0,
        ),
        name="finish",
    )(arrived, update)


def weight_grads_body(place_ref, *refs):
    gateacts, upacts = refs[:SIDE], refs[SIDE : 2 * SIDE]
    mine_ref, other_ref, grad_gate_ref, grad_up_ref, tokens, act = refs[2 * SIDE :]
    core = place_ref[1]
    chips, half, _ = mine_ref.shape
    width = 2 * half
    for chip in range(chips):
        own = pl.multiple_of(chip * width + core * half, half)
        their = pl.multiple_of(chip * width + (1 - core) * half, half)
        tokens[pl.ds(own, half), :] = mine_ref[chip]
        tokens[pl.ds(their, half), :] = other_ref[chip]
    for acts, out_ref in ((gateacts, grad_gate_ref), (upacts, grad_up_ref)):
        for number, offsets in enumerate(GROUPS):
            for k, offset in enumerate(offsets):
                start = pl.multiple_of(owner_of(place_ref, offset) * width, width)
                act[:, pl.ds(start, width)] = acts[number][:, k * width : (k + 1) * width]
        product = lax.dot_general(
            act[...], tokens[...], (((1,), (0,)), ((), ())), preferred_element_type=F32
        )
        out_ref[...] = (product * SCALE_WIDTH).astype(BF16)


def weight_grads(place, gateacts, upacts, mine, other):
    chips, half, depth = mine.shape
    units = gateacts[0].shape[0]
    tokens = chips * half * 2
    out = jax.ShapeDtypeStruct((units, depth), BF16)
    return pl.pallas_call(
        weight_grads_body,
        out_shape=[out, out],
        in_specs=[SMEM] + [VMEM] * (2 * SIDE + 2),
        out_specs=[VMEM] * 2,
        scratch_shapes=[pltpu.VMEM((tokens, depth), BF16), pltpu.VMEM((units, tokens), BF16)],
        compiler_params=params(),
        cost_estimate=pl.CostEstimate(
            flops=4 * units * depth * tokens,
            bytes_accessed=4 * units * tokens + 2 * tokens * depth + 4 * units * depth,
            transcendentals=0,
        ),
        name="weight_grads",
    )(place, *gateacts, *upacts, mine, other)


def shards(
    tokens, cotangent, gate_pre, up_act, gate_weight, up_weight, down_weight, moment_m, moment_v
):
    z = lax.axis_index("row")
    core = lax.axis_index("col") & 1
    place = jnp.stack([z, core, 1 - 2 * core]).astype(jnp.int32)

    acts = jnp.concatenate([gate_pre.T, up_act.T], axis=0)
    acts, cotangent = lax.optimization_barrier((acts, cotangent))
    acts = lax.all_gather(acts, "row", axis=0, tiled=False)
    cot_mine, cot_other = gather_chips(cotangent)
    cotangent_all, zero, far, odd, even, give_odd, give_even = hidden_partial(
        place, cot_mine, cot_other, down_weight
    )
    tokens, _ = lax.optimization_barrier((tokens, cot_other))
    tok_mine, tok_other = gather_chips(tokens)
    swish, slope, new_m, new_v, update, sums = down_update(
        acts, cotangent_all, down_weight, moment_m, moment_v
    )
    own, other = reduce_z(zero, far, odd, even, give_odd, give_even, sums)
    own, tok_other = lax.optimization_barrier((own, tok_other))

    gate_weight, up_weight = gate_weight.T, up_weight.T

    def group(number, grads, *befores):
        return input_group(
            number, place, grads, swish, slope, gate_weight, up_weight, *befores
        )

    others, owns = [other], [own]
    for _ in range(3):
        others.append(shift_z(others[-1], 2))
        owns.append(shift_z(owns[-1], 2))
    even_other, even = jnp.stack(others), jnp.stack(owns)
    odd_other = shift_z(even_other, 1)
    odd = shift_z(even, 1)
    far = shift_z(owns[3], 2)
    ahead_even = swap_core(even_other[1:])
    group_0 = group(0, (even,))
    group_1 = group(1, (ahead_even,), group_0[4], group_0[3])
    odd_other, odd, far, group_0, group_1 = lax.optimization_barrier(
        (odd_other, odd, far, group_0, group_1)
    )
    ahead_odd = swap_core(odd_other)
    group_2 = group(2, (odd,), group_1[4], group_1[3])
    group_3 = group(3, (ahead_odd, far), group_2[4])
    gateacts, upacts, mine, _, _ = zip(group_0, group_1, group_2, group_3)
    merged = merge_cores(
        place, mine, swap_core(group_2[3]), swap_core(group_3[3]), group_3[4]
    )
    merged, tok_mine = lax.optimization_barrier((merged, tok_mine))
    arrived = exchange_chips(merged)
    grad_gate, grad_up = weight_grads(place, gateacts, upacts, tok_mine, tok_other)
    arrived, grad_gate, grad_up = lax.optimization_barrier((arrived, grad_gate, grad_up))
    grad_input, step_down, ratio = finish(arrived, update)
    return grad_input, grad_gate.T, grad_up.T, new_m, new_v, step_down, ratio[0, 0]


def solution(mesh):
    in_specs = (
        P("col", "row"),
        P("col", "row"),
        P("row", "col"),
        P("row", "col"),
        P("row", "col"),
        P("row", "col"),
        P("col", "row"),
        P("col", "row"),
        P("col", "row"),
    )
    out_specs = (
        P("col", "row"),
        P("row", "col"),
        P("row", "col"),
        P("col", "row"),
        P("col", "row"),
        P("col", "row"),
        P(),
    )
    return jax.shard_map(shards, mesh=mesh, in_specs=in_specs, out_specs=out_specs, check_vma=False)
```

profile of v0, /device:TPU:1, one launch (start us, length us, event | category | flops | bytes accessed | tf_op | source)
XLA Modules:
  0.0 238.1 jit_solution(16086484391767626757)
XLA Ops:
  7.2 1.7 pad_maximum_fusion.3
  9.8 22.8 %all_to_all.15.mine_ref = bf16[16,64,512]{2,1,0:T(8,128)(2,1)S(1)} all-to-all(bf16[16,64,512]{2,1,0:T(8,128)(2,1)S(1)} %broadcast_in_dim.4), channel_id=1, replica_groups={{0,2,4,6,8,10,12,14,16,18,20,22,24,26,28,30},{1,3,5,7,9,11,13,15,17,19,..., dimensions={0} | all-to-all | bytes 2097152 | tf_op jit(solution)/shard_map/all_to_all | solution.py:43
  32.7 4.8 %collective-permute-start = (bf16[16,64,512]{2,1,0:T(8,128)(2,1)S(1)}, bf16[16,64,512]{2,1,0:T(8,128)(2,1)S(1)}, u32[]{:S(2)}, u32[]{:S(2)}) collective-permute-start(bf16[16,64,512]{2,1,0:T(8,128)(2,1)S(1)} %all_to_all.15.mine_ref), channel_id=1, source_target_pairs={{0,1},{1,0},{2,3},{3,2},{4,5},{5,4},{6,7},{7,6},{8,9},{9,8},{10,11... | collective-permute-start | bytes 3145736 | tf_op jit(solution)/shard_map/ppermute | solution.py:38
  37.6 2.2 collective-permute-done.other_ref
  39.8 1.0 copy-done.11
  40.8 1.0 copy-done.5
  41.8 1.2 copy-done.12
  43.0 3.1 %hidden_partial.1 = (bf16[2048,512]{1,0:T(8,128)(2,1)S(1)}, bf16[448,128]{1,0:T(8,128)(2,1)S(1)}, bf16[448,128]{1,0:T(8,128)(2,1)S(1)}, bf16[4,448,128]{2,1,0:T(...) custom-call(s32[3]{0:T(128)S(1)} %pad_add_fusion.place_ref, ...), custom_call_target="tpu_custom_call" | custom-call | flops 939524096 | bytes 6488064 | tf_op jit(solution)/shard_map/hidden_partial/pallas_call | solution.py:131
  46.8 2.3 collective-permute-start.2
  49.1 10.8 %collective-permute-start.6 = (bf16[4,448,128]{2,1,0:T(8,128)(2,1)}, bf16[4,448,128]{2,1,0:T(8,128)(2,1)}, u32[]{:S(2)}, u32[]{:S(2)}) collective-permute-start(bf16[4,448,128]{2,1,0:T(8,128)(2,1)} %get-tuple-element.73), channel_id=1, source_target_pairs={{0,32},{1,481},{2,34},{3,483},{4,36},{5,485},{6,38},{7,487},{8,40}... | collective-permute-start | bytes 1376264 | tf_op jit(solution)/shard_map/ppermute | solution.py:34
  60.0 2.6 %collective-permute-start.3 = (bf16[4,448,128]{2,1,0:T(8,128)(2,1)}, bf16[4,448,128]{2,1,0:T(8,128)(2,1)}, u32[]{:S(2)}, u32[]{:S(2)}) collective-permute-start(bf16[4,448,128]{2,1,0:T(8,128)(2,1)} %collective-permute-done.2), channel_id=1, source_target_pairs={{0,32},{1,481},{2,34},{3,483},{4,36},{5,485},{6,38},{7,487},{8,40}... | collective-permute-start | bytes 1376264 | tf_op jit(solution)/shard_map/ppermute | solution.py:34
  62.6 1.9 collective-permute-start.1
  64.5 2.0 broadcast_in_dim.5
  66.5 3.7 %all-to-all-start.1 = ((bf16[16,64,512]{2,1,0:T(8,128)(2,1)}), bf16[16,64,512]{2,1,0:T(8,128)(2,1)S(1)}, u32[]{:S(2)}, u32[]{:S(2)}) async-start(bf16[16,64,512]{2,1,0:T(8,128)(2,1)} %broadcast_in_dim.5), calls=%async_computation.1 | async-start | bytes 2097152 | tf_op jit(solution)/shard_map/all_to_all | solution.py:43
  70.2 5.2 %collective-permute-start.8 = (bf16[448,128]{1,0:T(8,128)(2,1)}, bf16[448,128]{1,0:T(8,128)(2,1)S(1)}, u32[]{:S(2)}, u32[]{:S(2)}) collective-permute-start(bf16[448,128]{1,0:T(8,128)(2,1)} %copy-done.27), channel_id=1, source_target_pairs={{0,128},{1,385},{2,130},{3,387},{4,132},{5,389},{6,134},{7,391},{8... | collective-permute-start | bytes 344072 | tf_op jit(solution)/shard_map/ppermute | solution.py:34
  76.3 3.8 %collective-permute-start.7 = (bf16[448,128]{1,0:T(8,128)(2,1)S(1)}, bf16[448,128]{1,0:T(8,128)(2,1)S(1)}, u32[]{:S(2)}, u32[]{:S(2)}) collective-permute-start(bf16[448,128]{1,0:T(8,128)(2,1)S(1)} %fusion.8), channel_id=1, source_target_pairs={{0,64},{1,449},{2,66},{3,451},{4,68},{5,453},{6,70},{7,455},{8,72}... | collective-permute-start | bytes 344072 | tf_op jit(solution)/shard_map/ppermute | solution.py:34
  80.1 12.1 %collective-permute-done.3 = bf16[4,448,128]{2,1,0:T(8,128)(2,1)} collective-permute-done((bf16[4,448,128]{2,1,0:T(8,128)(2,1)}, bf16[4,448,128]{2,1,0:T(8,128)(2,1)}, u32[]{:S(2)}, u32[]{:S(2)}) %collective-permute-start.3) | collective-permute-done | bytes 458784 | tf_op jit(solution)/shard_map/ppermute | solution.py:34
  93.2 1.9 collective-permute-start.4
  95.2 1.6 fusion.5
  96.8 6.1 %collective-permute-start.9 = (bf16[448,128]{1,0:T(8,128)(2,1)}, bf16[448,128]{1,0:T(8,128)(2,1)}, u32[]{:S(2)}, u32[]{:S(2)}) collective-permute-start(bf16[448,128]{1,0:T(8,128)(2,1)} %fusion.5), channel_id=1, source_target_pairs={{0,64},{1,449},{2,66},{3,451},{4,68},{5,453},{6,70},{7,455},{8,72}... | collective-permute-start | bytes 344072 | tf_op jit(solution)/shard_map/ppermute | solution.py:34
  102.9 1.6 fusion.6
  104.6 2.6 %collective-permute-start.5 = (bf16[448,128]{1,0:T(8,128)(2,1)}, bf16[448,128]{1,0:T(8,128)(2,1)}, u32[]{:S(2)}, u32[]{:S(2)}) collective-permute-start(bf16[448,128]{1,0:T(8,128)(2,1)} %fusion.6), channel_id=1, source_target_pairs={{0,64},{1,449},{2,66},{3,451},{4,68},{5,453},{6,70},{7,455},{8,72}... | collective-permute-start | bytes 344072 | tf_op jit(solution)/shard_map/ppermute | solution.py:34
  107.3 1.9 collective-permute-start.18
  109.2 2.0 copy-done.2
  111.3 1.0 copy-done.6
  112.3 1.0 copy-done.7
  113.3 1.0 copy-done.8
  114.3 6.0 %down_update.1 = (bf16[448,2048]{1,0:T(8,128)(2,1)S(1)}, bf16[448,2048]{1,0:T(8,128)(2,1)S(1)}, bf16[448,512]{1,0:T(8,128)(2,1)}, bf16[448,512]{1,0:T(8,128)(2,1...) custom-call(bf16[16,896,128]{2,1,0:T(8,128)(2,1)S(1)} %bitcast.78, ...), custom_call_target="tpu_custom_call" | custom-call | flops 967049216 | bytes 12648448 | tf_op jit(solution)/shard_map/down_update/pallas_call | solution.py:226
  120.3 1.4 fusion.3
  121.7 6.0 %collective-permute-start.10 = (bf16[448,128]{1,0:T(8,128)(2,1)S(1)}, bf16[448,128]{1,0:T(8,128)(2,1)S(1)}, u32[]{:S(2)}, u32[]{:S(2)}) collective-permute-start(bf16[448,128]{1,0:T(8,128)(2,1)S(1)} %fusion.3), channel_id=1, source_target_pairs={{0,64},{1,449},{2,66},{3,451},{4,68},{5,453},{6,70},{7,455},{8,72}... | collective-permute-start | bytes 344072 | tf_op jit(solution)/shard_map/ppermute | solution.py:34
  128.8 2.8 %collective-permute-start.11 = (bf16[448,128]{1,0:T(8,128)(2,1)S(1)}, bf16[448,128]{1,0:T(8,128)(2,1)S(1)}, u32[]{:S(2)}, u32[]{:S(2)}) collective-permute-start(bf16[448,128]{1,0:T(8,128)(2,1)S(1)} %fusion.1), channel_id=1, source_target_pairs={{0,64},{1,449},{2,66},{3,451},{4,68},{5,453},{6,70},{7,455},{8,72}... | collective-permute-start | bytes 344072 | tf_op jit(solution)/shard_map/ppermute | solution.py:34
  133.4 2.0 collective-permute-start.17
  135.4 1.0 collective-permute-done.11
  137.4 5.9 %collective-permute-start.12 = (bf16[464,128]{1,0:T(8,128)(2,1)S(1)}, bf16[464,128]{1,0:T(8,128)(2,1)S(1)}, u32[]{:S(2)}, u32[]{:S(2)}) collective-permute-start(bf16[464,128]{1,0:T(8,128)(2,1)S(1)} %pad_maximum_fusion.4), channel_id=1, source_target_pairs={{0,1},{1,0},{2,3},{3,2},{4,5},{5,4},{6,7},{7,6},{8,9},{9,8},{10,11... | collective-permute-start | bytes 356360 | tf_op jit(solution)/shard_map/ppermute | solution.py:38
  143.4 1.9 collective-permute-start.19
  145.4 3.4 %collective-permute-start.13 = (bf16[464,128]{1,0:T(8,128)(2,1)S(1)}, bf16[464,128]{1,0:T(8,128)(2,1)S(1)}, u32[]{:S(2)}, u32[]{:S(2)}) collective-permute-start(bf16[464,128]{1,0:T(8,128)(2,1)S(1)} %add_convert_fusion.1), channel_id=1, source_target_pairs={{0,64},{1,449},{2,66},{3,451},{4,68},{5,453},{6,70},{7,455},{8,72}... | collective-permute-start | bytes 356360 | tf_op jit(solution)/shard_map/ppermute | solution.py:34
  148.8 1.2 collective-permute-done.19
  150.0 4.4 %collective-permute-start.20 = (bf16[464,128]{1,0:T(8,128)(2,1)S(1)}, bf16[464,128]{1,0:T(8,128)(2,1)S(1)}, u32[]{:S(2)}, u32[]{:S(2)}) collective-permute-start(bf16[464,128]{1,0:T(8,128)(2,1)S(1)} %collective-permute-done.19), channel_id=1, source_target_pairs={{0,64},{1,449},{2,66},{3,451},{4,68},{5,453},{6,70},{7,455},{8,72}... | collective-permute-start | bytes 356360 | tf_op jit(solution)/shard_map/ppermute | solution.py:34
  154.4 3.4 %collective-permute-start.14 = (bf16[464,128]{1,0:T(8,128)(2,1)S(1)}, bf16[464,128]{1,0:T(8,128)(2,1)S(1)}, u32[]{:S(2)}, u32[]{:S(2)}) collective-permute-start(bf16[464,128]{1,0:T(8,128)(2,1)S(1)} %collective-permute-done.13), channel_id=1, source_target_pairs={{0,64},{1,449},{2,66},{3,451},{4,68},{5,453},{6,70},{7,455},{8,72}... | collective-permute-start | bytes 356360 | tf_op jit(solution)/shard_map/ppermute | solution.py:34
  157.8 4.6 %collective-permute-start.21 = (bf16[464,128]{1,0:T(8,128)(2,1)S(1)}, bf16[464,128]{1,0:T(8,128)(2,1)S(1)}, u32[]{:S(2)}, u32[]{:S(2)}) collective-permute-start(bf16[464,128]{1,0:T(8,128)(2,1)S(1)} %collective-permute-done.20), channel_id=1, source_target_pairs={{0,64},{1,449},{2,66},{3,451},{4,68},{5,453},{6,70},{7,455},{8,72}... | collective-permute-start | bytes 356360 | tf_op jit(solution)/shard_map/ppermute | solution.py:34
  162.4 3.8 %collective-permute-start.15 = (bf16[464,128]{1,0:T(8,128)(2,1)S(1)}, bf16[464,128]{1,0:T(8,128)(2,1)S(1)}, u32[]{:S(2)}, u32[]{:S(2)}) collective-permute-start(bf16[464,128]{1,0:T(8,128)(2,1)S(1)} %collective-permute-done.14), channel_id=1, source_target_pairs={{0,64},{1,449},{2,66},{3,451},{4,68},{5,453},{6,70},{7,455},{8,72}... | collective-permute-start | bytes 356360 | tf_op jit(solution)/shard_map/ppermute | solution.py:34
  166.3 3.1 %collective-permute-start.22 = (bf16[4,464,128]{2,1,0:T(8,128)(2,1)S(1)}, bf16[4,464,128]{2,1,0:T(8,128)(2,1)S(1)}, u32[]{:S(2)}, u32[]{:S(2)}) collective-permute-start(bf16[4,464,128]{2,1,0:T(8,128)(2,1)S(1)} %pad_maximum_fusion.1.refs_0_), channel_id=1, source_target_pairs={{0,32},{1,481},{2,34},{3,483},{4,36},{5,485},{6,38},{7,487},{8,40}... | collective-permute-start | bytes 1425416 | tf_op jit(solution)/shard_map/ppermute | solution.py:34
  169.9 3.4 %collective-permute-start.16 = (bf16[4,464,128]{2,1,0:T(8,128)(2,1)S(1)}, bf16[4,464,128]{2,1,0:T(8,128)(2,1)S(1)}, u32[]{:S(2)}, u32[]{:S(2)}) collective-permute-start(bf16[4,464,128]{2,1,0:T(8,128)(2,1)S(1)} %pad_maximum_fusion), channel_id=1, source_target_pairs={{0,32},{1,481},{2,34},{3,483},{4,36},{5,485},{6,38},{7,487},{8,40}... | collective-permute-start | bytes 1425416 | tf_op jit(solution)/shard_map/ppermute | solution.py:34
  173.3 8.0 %collective-permute-start.24 = (bf16[3,464,128]{2,1,0:T(8,128)(2,1)S(1)}, bf16[3,464,128]{2,1,0:T(8,128)(2,1)S(1)}, u32[]{:S(2)}, u32[]{:S(2)}) collective-permute-start(bf16[3,464,128]{2,1,0:T(8,128)(2,1)S(1)} %pad_maximum_fusion.2), channel_id=1, source_target_pairs={{0,1},{1,0},{2,3},{3,2},{4,5},{5,4},{6,7},{7,6},{8,9},{9,8},{10,11... | collective-permute-start | bytes 1069064 | tf_op jit(solution)/shard_map/ppermute | solution.py:38
  181.3 4.4 %collective-permute-start.23 = (bf16[464,128]{1,0:T(8,128)(2,1)S(1)}, bf16[464,128]{1,0:T(8,128)(2,1)S(1)}, u32[]{:S(2)}, u32[]{:S(2)}) collective-permute-start(bf16[464,128]{1,0:T(8,128)(2,1)S(1)} %collective-permute-done.21), channel_id=1, source_target_pairs={{0,64},{1,449},{2,66},{3,451},{4,68},{5,453},{6,70},{7,455},{8,72}... | collective-permute-start | bytes 356360 | tf_op jit(solution)/shard_map/ppermute | solution.py:34
  185.7 1.8 input_group.4
  188.3 1.5 input_group.5
  190.6 3.0 %collective-permute-start.25 = (bf16[4,464,128]{2,1,0:T(8,128)(2,1)S(1)}, bf16[4,464,128]{2,1,0:T(8,128)(2,1)S(1)}, u32[]{:S(2)}, u32[]{:S(2)}) collective-permute-start(bf16[4,464,128]{2,1,0:T(8,128)(2,1)S(1)} %collective-permute-done.16), channel_id=1, source_target_pairs={{0,1},{1,0},{2,3},{3,2},{4,5},{5,4},{6,7},{7,6},{8,9},{9,8},{10,11... | collective-permute-start | bytes 1425416 | tf_op jit(solution)/shard_map/ppermute | solution.py:38
  193.5 1.8 input_group.6
  196.1 1.9 collective-permute-start.26
  198.0 2.0 input_group.7
  201.7 2.4 %collective-permute-start.27 = (bf16[336,512]{1,0:T(8,128)(2,1)S(1)}, bf16[336,512]{1,0:T(8,128)(2,1)S(1)}, u32[]{:S(2)}, u32[]{:S(2)}) collective-permute-start(bf16[336,512]{1,0:T(8,128)(2,1)S(1)} %get-tuple-element.107), channel_id=1, source_target_pairs={{0,1},{1,0},{2,3},{3,2},{4,5},{5,4},{6,7},{7,6},{8,9},{9,8},{10,11... | collective-permute-start | bytes 1032200 | tf_op jit(solution)/shard_map/ppermute | solution.py:38
  204.1 1.2 collective-permute-done.27.refs_5_
  205.3 2.0 merge_cores.1
  207.4 3.9 %all-to-all-start.2 = ((bf16[16,272,128]{2,1,0:T(8,128)(2,1)}), bf16[16,272,128]{2,1,0:T(8,128)(2,1)S(1)}, u32[]{:S(2)}, u32[]{:S(2)}) async-start(bf16[16,272,128]{2,1,0:T(8,128)(2,1)} %merge_cores.1), calls=%async_computation.2 | async-start | bytes 2228224 | tf_op jit(solution)/shard_map/all_to_all | solution.py:43
  211.3 1.1 copy-done.14
  212.3 1.1 copy-done.16
  213.4 1.0 copy-done.18
  214.4 1.0 copy-done.20
  215.4 1.0 copy-done.22
  216.5 1.0 copy-done.24
  218.5 5.3 %weight_grads.1 = (bf16[448,512]{1,0:T(8,128)(2,1)}, bf16[448,512]{1,0:T(8,128)(2,1)}) custom-call(s32[3]{0:T(128)S(1)} %pad_add_fusion.place_ref, bf16[448,512]{1,0:T(8,128)(2,1)S(1)} %copy-done.18, bf16[448,384]{1,0:T(8,128)(2,1)S(1)} %get-tuple-element.111.refs_1_, bf16[448,512]{1,0:T(8,128)(2,1)S(1)} %copy-done.22, bf16[448,640]{1,0:T(8,128)(2,1)S(1)} %copy-done.14, ...), custom_call_target="tpu_custom_call" | custom-call | flops 1879048192 | bytes 6684672 | tf_op jit(solution)/shard_map/weight_grads/pallas_call | solution.py:444
  223.7 5.5 %all-to-all-done.2.arrived_ref = bf16[16,272,128]{2,1,0:T(8,128)(2,1)S(1)} async-done(((bf16[16,272,128]{2,1,0:T(8,128)(2,1)}), bf16[16,272,128]{2,1,0:T(8,128)(2,1)S(1)}, u32[]{:S(2)}, u32[]{:S(2)}) %all-to-all-start.2) | async-done | bytes 1114144 | tf_op jit(solution)/shard_map/all_to_all | solution.py:43
  229.2 2.0 finish.1
  (84 shorter events, 13.1 us)
Async XLA Ops:
  7.2 102.0 %all-gather.3.cloned.1.call-start = ((), (), s32[]{:S(2)}) async-start(), calls=%async_computation.3 | async-start | bytes 3899392 | tf_op jit(solution)/shard_map/all_gather | solution.py:469
  32.7 7.1 %collective-permute-start = (bf16[16,64,512]{2,1,0:T(8,128)(2,1)S(1)}, bf16[16,64,512]{2,1,0:T(8,128)(2,1)S(1)}, u32[]{:S(2)}, u32[]{:S(2)}) collective-permute-start(bf16[16,64,512]{2,1,0:T(8,128)(2,1)S(1)} %all_to_all.15.mine_ref), channel_id=1, source_target_pairs={{0,1},{1,0},{2,3},{3,2},{4,5},{5,4},{6,7},{7,6},{8,9},{9,8},{10,11... | collective-permute-start | bytes 3145736 | tf_op jit(solution)/shard_map/ppermute | solution.py:38
  39.8 1.0 copy-start.11
  40.8 1.0 copy-start.5
  41.8 1.2 copy-start.12
  46.2 0.6 copy-start.9
  46.8 13.1 %copy-start.27 = (bf16[448,128]{1,0:T(8,128)(2,1)}, bf16[448,128]{1,0:T(8,128)(2,1)S(1)}, u32[]{:S(2)}) copy-start(bf16[448,128]{1,0:T(8,128)(2,1)S(1)} %get-tuple-element.74) | copy-start | bytes 344068
  46.8 13.1 %collective-permute-start.2 = (bf16[4,448,128]{2,1,0:T(8,128)(2,1)S(1)}, bf16[4,448,128]{2,1,0:T(8,128)(2,1)}, u32[]{:S(2)}, u32[]{:S(2)}) collective-permute-start(bf16[4,448,128]{2,1,0:T(8,128)(2,1)S(1)} %get-tuple-element.71), channel_id=1, source_target_pairs={{0,1},{1,0},{2,3},{3,2},{4,5},{5,4},{6,7},{7,6},{8,9},{9,8},{10,11... | collective-permute-start | bytes 1376264 | tf_op jit(solution)/shard_map/ppermute | solution.py:38
  49.1 26.3 %collective-permute-start.6 = (bf16[4,448,128]{2,1,0:T(8,128)(2,1)}, bf16[4,448,128]{2,1,0:T(8,128)(2,1)}, u32[]{:S(2)}, u32[]{:S(2)}) collective-permute-start(bf16[4,448,128]{2,1,0:T(8,128)(2,1)} %get-tuple-element.73), channel_id=1, source_target_pairs={{0,32},{1,481},{2,34},{3,483},{4,36},{5,485},{6,38},{7,487},{8,40}... | collective-permute-start | bytes 1376264 | tf_op jit(solution)/shard_map/ppermute | solution.py:34
  60.0 32.3 %collective-permute-start.3 = (bf16[4,448,128]{2,1,0:T(8,128)(2,1)}, bf16[4,448,128]{2,1,0:T(8,128)(2,1)}, u32[]{:S(2)}, u32[]{:S(2)}) collective-permute-start(bf16[4,448,128]{2,1,0:T(8,128)(2,1)} %collective-permute-done.2), channel_id=1, source_target_pairs={{0,32},{1,481},{2,34},{3,483},{4,36},{5,485},{6,38},{7,487},{8,40}... | collective-permute-start | bytes 1376264 | tf_op jit(solution)/shard_map/ppermute | solution.py:34
  62.6 17.5 %collective-permute-start.1 = (bf16[3,448,128]{2,1,0:T(8,128)(2,1)}, bf16[3,448,128]{2,1,0:T(8,128)(2,1)}, u32[]{:S(2)}, u32[]{:S(2)}) collective-permute-start(bf16[3,448,128]{2,1,0:T(8,128)(2,1)} %get-tuple-element.70), channel_id=1, source_target_pairs={{0,1},{1,0},{2,3},{3,2},{4,5},{5,4},{6,7},{7,6},{8,9},{9,8},{10,11... | collective-permute-start | bytes 1032200 | tf_op jit(solution)/shard_map/ppermute | solution.py:38
  66.5 40.7 %all-to-all-start.1 = ((bf16[16,64,512]{2,1,0:T(8,128)(2,1)}), bf16[16,64,512]{2,1,0:T(8,128)(2,1)S(1)}, u32[]{:S(2)}, u32[]{:S(2)}) async-start(bf16[16,64,512]{2,1,0:T(8,128)(2,1)} %broadcast_in_dim.5), calls=%async_computation.1 | async-start | bytes 2097152 | tf_op jit(solution)/shard_map/all_to_all | solution.py:43
  70.2 25.0 %collective-permute-start.8 = (bf16[448,128]{1,0:T(8,128)(2,1)}, bf16[448,128]{1,0:T(8,128)(2,1)S(1)}, u32[]{:S(2)}, u32[]{:S(2)}) collective-permute-start(bf16[448,128]{1,0:T(8,128)(2,1)} %copy-done.27), channel_id=1, source_target_pairs={{0,128},{1,385},{2,130},{3,387},{4,132},{5,389},{6,134},{7,391},{8... | collective-permute-start | bytes 344072 | tf_op jit(solution)/shard_map/ppermute | solution.py:34
  76.3 18.9 %collective-permute-start.7 = (bf16[448,128]{1,0:T(8,128)(2,1)S(1)}, bf16[448,128]{1,0:T(8,128)(2,1)S(1)}, u32[]{:S(2)}, u32[]{:S(2)}) collective-permute-start(bf16[448,128]{1,0:T(8,128)(2,1)S(1)} %fusion.8), channel_id=1, source_target_pairs={{0,64},{1,449},{2,66},{3,451},{4,68},{5,453},{6,70},{7,455},{8,72}... | collective-permute-start | bytes 344072 | tf_op jit(solution)/shard_map/ppermute | solution.py:34
  93.2 9.7 %collective-permute-start.4 = (bf16[448,128]{1,0:T(8,128)(2,1)S(1)}, bf16[448,128]{1,0:T(8,128)(2,1)S(1)}, u32[]{:S(2)}, u32[]{:S(2)}) collective-permute-start(bf16[448,128]{1,0:T(8,128)(2,1)S(1)} %fusion.7), channel_id=1, source_target_pairs={{0,64},{1,449},{2,66},{3,451},{4,68},{5,453},{6,70},{7,455},{8,72}... | collective-permute-start | bytes 344072 | tf_op jit(solution)/shard_map/ppermute | solution.py:34
  96.8 23.5 %collective-permute-start.9 = (bf16[448,128]{1,0:T(8,128)(2,1)}, bf16[448,128]{1,0:T(8,128)(2,1)}, u32[]{:S(2)}, u32[]{:S(2)}) collective-permute-start(bf16[448,128]{1,0:T(8,128)(2,1)} %fusion.5), channel_id=1, source_target_pairs={{0,64},{1,449},{2,66},{3,451},{4,68},{5,453},{6,70},{7,455},{8,72}... | collective-permute-start | bytes 344072 | tf_op jit(solution)/shard_map/ppermute | solution.py:34
  104.6 15.7 %collective-permute-start.5 = (bf16[448,128]{1,0:T(8,128)(2,1)}, bf16[448,128]{1,0:T(8,128)(2,1)}, u32[]{:S(2)}, u32[]{:S(2)}) collective-permute-start(bf16[448,128]{1,0:T(8,128)(2,1)} %fusion.6), channel_id=1, source_target_pairs={{0,64},{1,449},{2,66},{3,451},{4,68},{5,453},{6,70},{7,455},{8,72}... | collective-permute-start | bytes 344072 | tf_op jit(solution)/shard_map/ppermute | solution.py:34
  107.3 36.2 %collective-permute-start.18 = (bf16[16,64,512]{2,1,0:T(8,128)(2,1)S(1)}, bf16[16,64,512]{2,1,0:T(8,128)(2,1)}, u32[]{:S(2)}, u32[]{:S(2)}) collective-permute-start(bf16[16,64,512]{2,1,0:T(8,128)(2,1)S(1)} %all-to-all-done.1.refs_8_), channel_id=1, source_target_pairs={{0,1},{1,0},{2,3},{3,2},{4,5},{5,4},{6,7},{7,6},{8,9},{9,8},{10,11... | collective-permute-start | bytes 3145736 | tf_op jit(solution)/shard_map/ppermute | solution.py:38
  109.2 2.0 copy-start.2
  111.3 1.0 copy-start.6
  112.3 1.0 copy-start.7
  113.3 1.0 copy-start.8
  114.3 22.1 %copy-start.10 = (bf16[448,128]{1,0:T(8,128)(2,1)S(1)}, bf16[448,128]{1,0:T(8,128)(2,1)}, u32[]{:S(2)}) copy-start(bf16[448,128]{1,0:T(8,128)(2,1)} %copy-done.9) | copy-start | bytes 344068
  120.3 46.0 %copy-start.3 = (f32[448,512]{1,0:T(8,128)}, f32[448,512]{1,0:T(8,128)S(1)}, u32[]{:S(2)}) copy-start(f32[448,512]{1,0:T(8,128)S(1)} %get-tuple-element.123.update_ref) | copy-start | bytes 2752516
  121.7 10.7 %collective-permute-start.10 = (bf16[448,128]{1,0:T(8,128)(2,1)S(1)}, bf16[448,128]{1,0:T(8,128)(2,1)S(1)}, u32[]{:S(2)}, u32[]{:S(2)}) collective-permute-start(bf16[448,128]{1,0:T(8,128)(2,1)S(1)} %fusion.3), channel_id=1, source_target_pairs={{0,64},{1,449},{2,66},{3,451},{4,68},{5,453},{6,70},{7,455},{8,72}... | collective-permute-start | bytes 344072 | tf_op jit(solution)/shard_map/ppermute | solution.py:34
  128.8 7.7 %collective-permute-start.11 = (bf16[448,128]{1,0:T(8,128)(2,1)S(1)}, bf16[448,128]{1,0:T(8,128)(2,1)S(1)}, u32[]{:S(2)}, u32[]{:S(2)}) collective-permute-start(bf16[448,128]{1,0:T(8,128)(2,1)S(1)} %fusion.1), channel_id=1, source_target_pairs={{0,64},{1,449},{2,66},{3,451},{4,68},{5,453},{6,70},{7,455},{8,72}... | collective-permute-start | bytes 344072 | tf_op jit(solution)/shard_map/ppermute | solution.py:34
  133.4 10.0 %collective-permute-start.17 = (bf16[464,128]{1,0:T(8,128)(2,1)S(1)}, bf16[464,128]{1,0:T(8,128)(2,1)S(1)}, u32[]{:S(2)}, u32[]{:S(2)}) collective-permute-start(bf16[464,128]{1,0:T(8,128)(2,1)S(1)} %concatenate.11), channel_id=1, source_target_pairs={{0,1},{1,0},{2,3},{3,2},{4,5},{5,4},{6,7},{7,6},{8,9},{9,8},{10,11... | collective-permute-start | bytes 356360 | tf_op jit(solution)/shard_map/ppermute | solution.py:38
  137.4 48.3 %copy-start = (bf16[512,448]{0,1:T(8,128)(2,1)S(1)}, bf16[512,448]{0,1:T(8,128)(2,1)}, u32[]{:S(2)}) copy-start(bf16[512,448]{0,1:T(8,128)(2,1)} %param.13) | copy-start | bytes 1376260
  137.4 48.3 %copy-start.1 = (bf16[512,448]{0,1:T(8,128)(2,1)S(1)}, bf16[512,448]{0,1:T(8,128)(2,1)}, u32[]{:S(2)}) copy-start(bf16[512,448]{0,1:T(8,128)(2,1)} %param.14) | copy-start | bytes 1376260
  137.4 7.9 %collective-permute-start.12 = (bf16[464,128]{1,0:T(8,128)(2,1)S(1)}, bf16[464,128]{1,0:T(8,128)(2,1)S(1)}, u32[]{:S(2)}, u32[]{:S(2)}) collective-permute-start(bf16[464,128]{1,0:T(8,128)(2,1)S(1)} %pad_maximum_fusion.4), channel_id=1, source_target_pairs={{0,1},{1,0},{2,3},{3,2},{4,5},{5,4},{6,7},{7,6},{8,9},{9,8},{10,11... | collective-permute-start | bytes 356360 | tf_op jit(solution)/shard_map/ppermute | solution.py:38
  143.4 6.5 %collective-permute-start.19 = (bf16[464,128]{1,0:T(8,128)(2,1)S(1)}, bf16[464,128]{1,0:T(8,128)(2,1)S(1)}, u32[]{:S(2)}, u32[]{:S(2)}) collective-permute-start(bf16[464,128]{1,0:T(8,128)(2,1)S(1)} %add_convert_fusion), channel_id=1, source_target_pairs={{0,64},{1,449},{2,66},{3,451},{4,68},{5,453},{6,70},{7,455},{8,72}... | collective-permute-start | bytes 356360 | tf_op jit(solution)/shard_map/ppermute | solution.py:34
  145.4 8.9 %collective-permute-start.13 = (bf16[464,128]{1,0:T(8,128)(2,1)S(1)}, bf16[464,128]{1,0:T(8,128)(2,1)S(1)}, u32[]{:S(2)}, u32[]{:S(2)}) collective-permute-start(bf16[464,128]{1,0:T(8,128)(2,1)S(1)} %add_convert_fusion.1), channel_id=1, source_target_pairs={{0,64},{1,449},{2,66},{3,451},{4,68},{5,453},{6,70},{7,455},{8,72}... | collective-permute-start | bytes 356360 | tf_op jit(solution)/shard_map/ppermute | solution.py:34
  150.0 7.8 %collective-permute-start.20 = (bf16[464,128]{1,0:T(8,128)(2,1)S(1)}, bf16[464,128]{1,0:T(8,128)(2,1)S(1)}, u32[]{:S(2)}, u32[]{:S(2)}) collective-permute-start(bf16[464,128]{1,0:T(8,128)(2,1)S(1)} %collective-permute-done.19), channel_id=1, source_target_pairs={{0,64},{1,449},{2,66},{3,451},{4,68},{5,453},{6,70},{7,455},{8,72}... | collective-permute-start | bytes 356360 | tf_op jit(solution)/shard_map/ppermute | solution.py:34
  154.4 8.0 %collective-permute-start.14 = (bf16[464,128]{1,0:T(8,128)(2,1)S(1)}, bf16[464,128]{1,0:T(8,128)(2,1)S(1)}, u32[]{:S(2)}, u32[]{:S(2)}) collective-permute-start(bf16[464,128]{1,0:T(8,128)(2,1)S(1)} %collective-permute-done.13), channel_id=1, source_target_pairs={{0,64},{1,449},{2,66},{3,451},{4,68},{5,453},{6,70},{7,455},{8,72}... | collective-permute-start | bytes 356360 | tf_op jit(solution)/shard_map/ppermute | solution.py:34
  157.8 8.4 %collective-permute-start.21 = (bf16[464,128]{1,0:T(8,128)(2,1)S(1)}, bf16[464,128]{1,0:T(8,128)(2,1)S(1)}, u32[]{:S(2)}, u32[]{:S(2)}) collective-permute-start(bf16[464,128]{1,0:T(8,128)(2,1)S(1)} %collective-permute-done.20), channel_id=1, source_target_pairs={{0,64},{1,449},{2,66},{3,451},{4,68},{5,453},{6,70},{7,455},{8,72}... | collective-permute-start | bytes 356360 | tf_op jit(solution)/shard_map/ppermute | solution.py:34
  162.4 7.4 %collective-permute-start.15 = (bf16[464,128]{1,0:T(8,128)(2,1)S(1)}, bf16[464,128]{1,0:T(8,128)(2,1)S(1)}, u32[]{:S(2)}, u32[]{:S(2)}) collective-permute-start(bf16[464,128]{1,0:T(8,128)(2,1)S(1)} %collective-permute-done.14), channel_id=1, source_target_pairs={{0,64},{1,449},{2,66},{3,451},{4,68},{5,453},{6,70},{7,455},{8,72}... | collective-permute-start | bytes 356360 | tf_op jit(solution)/shard_map/ppermute | solution.py:34
  166.3 24.3 %collective-permute-start.22 = (bf16[4,464,128]{2,1,0:T(8,128)(2,1)S(1)}, bf16[4,464,128]{2,1,0:T(8,128)(2,1)S(1)}, u32[]{:S(2)}, u32[]{:S(2)}) collective-permute-start(bf16[4,464,128]{2,1,0:T(8,128)(2,1)S(1)} %pad_maximum_fusion.1.refs_0_), channel_id=1, source_target_pairs={{0,32},{1,481},{2,34},{3,483},{4,36},{5,485},{6,38},{7,487},{8,40}... | collective-permute-start | bytes 1425416 | tf_op jit(solution)/shard_map/ppermute | solution.py:34
  169.9 20.7 %collective-permute-start.16 = (bf16[4,464,128]{2,1,0:T(8,128)(2,1)S(1)}, bf16[4,464,128]{2,1,0:T(8,128)(2,1)S(1)}, u32[]{:S(2)}, u32[]{:S(2)}) collective-permute-start(bf16[4,464,128]{2,1,0:T(8,128)(2,1)S(1)} %pad_maximum_fusion), channel_id=1, source_target_pairs={{0,32},{1,481},{2,34},{3,483},{4,36},{5,485},{6,38},{7,487},{8,40}... | collective-permute-start | bytes 1425416 | tf_op jit(solution)/shard_map/ppermute | solution.py:34
  173.3 15.0 %collective-permute-start.24 = (bf16[3,464,128]{2,1,0:T(8,128)(2,1)S(1)}, bf16[3,464,128]{2,1,0:T(8,128)(2,1)S(1)}, u32[]{:S(2)}, u32[]{:S(2)}) collective-permute-start(bf16[3,464,128]{2,1,0:T(8,128)(2,1)S(1)} %pad_maximum_fusion.2), channel_id=1, source_target_pairs={{0,1},{1,0},{2,3},{3,2},{4,5},{5,4},{6,7},{7,6},{8,9},{9,8},{10,11... | collective-permute-start | bytes 1069064 | tf_op jit(solution)/shard_map/ppermute | solution.py:38
  181.3 9.2 %collective-permute-start.23 = (bf16[464,128]{1,0:T(8,128)(2,1)S(1)}, bf16[464,128]{1,0:T(8,128)(2,1)S(1)}, u32[]{:S(2)}, u32[]{:S(2)}) collective-permute-start(bf16[464,128]{1,0:T(8,128)(2,1)S(1)} %collective-permute-done.21), channel_id=1, source_target_pairs={{0,64},{1,449},{2,66},{3,451},{4,68},{5,453},{6,70},{7,455},{8,72}... | collective-permute-start | bytes 356360 | tf_op jit(solution)/shard_map/ppermute | solution.py:34
  187.5 0.8 copy-start.19
  188.3 1.5 copy-start.17
  189.8 0.7 copy-start.25
  190.6 7.5 %collective-permute-start.25 = (bf16[4,464,128]{2,1,0:T(8,128)(2,1)S(1)}, bf16[4,464,128]{2,1,0:T(8,128)(2,1)S(1)}, u32[]{:S(2)}, u32[]{:S(2)}) collective-permute-start(bf16[4,464,128]{2,1,0:T(8,128)(2,1)S(1)} %collective-permute-done.16), channel_id=1, source_target_pairs={{0,1},{1,0},{2,3},{3,2},{4,5},{5,4},{6,7},{7,6},{8,9},{9,8},{10,11... | collective-permute-start | bytes 1425416 | tf_op jit(solution)/shard_map/ppermute | solution.py:38
  195.3 0.8 copy-start.23
  196.1 4.0 %copy-start.21 = (bf16[448,512]{1,0:T(8,128)(2,1)}, bf16[448,512]{1,0:T(8,128)(2,1)S(1)}, u32[]{:S(2)}) copy-start(bf16[448,512]{1,0:T(8,128)(2,1)S(1)} %get-tuple-element.112.refs_2_) | copy-start | bytes 1376260
  196.1 8.0 %collective-permute-start.26 = (bf16[704,512]{1,0:T(8,128)(2,1)S(1)}, bf16[704,512]{1,0:T(8,128)(2,1)S(1)}, u32[]{:S(2)}, u32[]{:S(2)}) collective-permute-start(bf16[704,512]{1,0:T(8,128)(2,1)S(1)} %get-tuple-element.106), channel_id=1, source_target_pairs={{0,1},{1,0},{2,3},{3,2},{4,5},{5,4},{6,7},{7,6},{8,9},{9,8},{10,11... | collective-permute-start | bytes 2162696 | tf_op jit(solution)/shard_map/ppermute | solution.py:38
  200.1 0.8 copy-start.13
  200.9 0.8 copy-start.15
  201.7 3.7 %collective-permute-start.27 = (bf16[336,512]{1,0:T(8,128)(2,1)S(1)}, bf16[336,512]{1,0:T(8,128)(2,1)S(1)}, u32[]{:S(2)}, u32[]{:S(2)}) collective-permute-start(bf16[336,512]{1,0:T(8,128)(2,1)S(1)} %get-tuple-element.107), channel_id=1, source_target_pairs={{0,1},{1,0},{2,3},{3,2},{4,5},{5,4},{6,7},{7,6},{8,9},{9,8},{10,11... | collective-permute-start | bytes 1032200 | tf_op jit(solution)/shard_map/ppermute | solution.py:38
  207.4 21.9 %all-to-all-start.2 = ((bf16[16,272,128]{2,1,0:T(8,128)(2,1)}), bf16[16,272,128]{2,1,0:T(8,128)(2,1)S(1)}, u32[]{:S(2)}, u32[]{:S(2)}) async-start(bf16[16,272,128]{2,1,0:T(8,128)(2,1)} %merge_cores.1), calls=%async_computation.2 | async-start | bytes 2228224 | tf_op jit(solution)/shard_map/all_to_all | solution.py:43
  211.3 1.1 copy-start.14
  212.3 1.1 copy-start.16
  213.4 1.0 copy-start.18
  214.4 1.0 copy-start.20
  215.4 1.0 copy-start.22
  216.5 1.0 copy-start.24
  217.5 1.0 copy-start.26
  218.5 10.8 %copy-start.4 = (f32[448,512]{1,0:T(8,128)S(1)}, f32[448,512]{1,0:T(8,128)}, u32[]{:S(2)}) copy-start(f32[448,512]{1,0:T(8,128)} %copy-done.3) | copy-start | bytes 2752516
Sparse Core Ops, SparseCore 0:
  10.7 85.1 all-gather.2
where the time goes:
time: 241 us; the launch traced here: 238 us
  starting transfers between devices  116 us (48%)
  Pallas kernels  25.5 us (11%)
  waiting for transfers between devices  24.7 us (10%)
  local copies, waits for them, and re-layouts  23 us (10%)
  blocking collectives  22.8 us (9%)
  between operations  14.7 us (6%)
  other arithmetic  11.4 us (5%)
    ppermute x18, starting transfers between devices, shift_z(): return lax.ppermute(v, ('row', 'col'), pairs)  74.3 us
    ppermute x10, starting transfers between devices, swap_core(): return lax.ppermute(v, 'col', [(c, c ^ 1) for c in range(COLS)])  34.1 us
    all_to_all x1, blocking collectives, exchange_chips(): return lax.all_to_all(v, 'col', 0, 0, axis_index_groups=groups, tiled=True)  22.8 us
    unnamed x56, local copies, waits for them, and re-layouts  20.1 us
    ppermute x18, waiting for transfers between devices, shift_z(): return lax.ppermute(v, ('row', 'col'), pairs)  15.7 us
    convert_element_type x10, other arithmetic, add(): return total.astype(BF16)  9.53 us
    all_to_all x2, starting transfers between devices, exchange_chips(): return lax.all_to_all(v, 'col', 0, 0, axis_index_groups=groups, tiled=True)  7.53 us
    pallas_call x4, Pallas kernels, input_group(): pl.pallas_call(functools.partial(group_body, number, len(grads)), out_sha...  7.08 us
  transfers between devices with their start and end apart: 31, of which 8 were waited for; matrix products, arithmetic and copies ran while one was open for 5% of the time, Pallas kernels for 9%

commit v1 on v0

--- a/solution.py
+++ b/solution.py
@@ -43,11 +43,6 @@
     return lax.all_to_all(v, "col", 0, 0, axis_index_groups=groups, tiled=True)
 
 
-def gather_chips(v):
-    mine = exchange_chips(jnp.broadcast_to(v[None], (CHIPS, *v.shape)))
-    return mine, swap_core(mine)
-
-
 def add(*terms):
     total = terms[0].astype(F32)
     for term in terms[1:]:
@@ -55,28 +50,24 @@
     return total.astype(BF16)
 
 
-def reduce_z(zero, far, odd, even, give_odd, give_even, extra):
-    own = shift_z(odd, 1)
-    got_odd = swap_core(give_odd)
-    their = shift_z(got_odd, 1)
-    far = shift_z(far, SIDE)
-    got_even = swap_core(give_even)
-    moving_their = add(got_even[2], their[3])
-    moving = add(even[2], own[3])
-    for k in (2, 1):
-        moving_their = shift_z(moving_their, 2)
-        moving = shift_z(moving, 2)
+def reduce_z(zero, far, ahead, give, first_ready, second_ready):
+    their = swap_core(give)
+    moving = shift_z(far, 1)
+    moving = shift_z(add(moving, ahead[6]), 1)
+    moving_their = shift_z(their[6], 1)
+    for k in range(5, -1, -1):
         if k == 1:
-            moving_their, moving, extra = lax.optimization_barrier((moving_their, moving, extra))
-        moving_their = add(moving_their, got_even[k - 1], their[k])
-        moving = add(moving, even[k - 1], own[k], *([far] if k == 2 else []))
-    moving_their = shift_z(moving_their, 2)
-    moving = shift_z(moving, 2)
-    other = jnp.concatenate([add(moving_their, their[0]), jnp.zeros_like(extra)], axis=0)
-    mine = jnp.concatenate([add(zero, moving, own[0]), extra], axis=0)
+            moving, moving_their, first_ready = lax.optimization_barrier(
+                (moving, moving_their, first_ready)
+            )
+        moving_their = shift_z(add(moving_their, their[k]), 1)
+        moving = shift_z(add(moving, ahead[k]), 1)
+    moving, moving_their, extra = lax.optimization_barrier((moving, moving_their, second_ready))
+    other = jnp.concatenate([moving_their, jnp.zeros_like(extra)], axis=0)
+    mine = jnp.concatenate([add(zero, moving), extra], axis=0)
     got_mine = swap_core(other)
     got_other = swap_core(mine)
-    return add(mine, got_mine), add(other, got_other)
+    return add(mine, got_mine), add(other, got_other), first_ready
 
 
 GROUPS = ((0, -2, -4, -6), (2, 4, 6), (-1, -3, -5, -7), (1, 3, 5, 7, -8))
@@ -88,7 +79,7 @@
 
 
 def hidden_partial_body(place_ref, mine_ref, other_ref, weight_ref, cot_ref, *refs):
-    zero_ref, far_ref, odd_ref, even_ref, give_odd_ref, give_even_ref, hold = refs
+    zero_ref, far_ref, ahead_ref, give_ref, hold = refs
     core = place_ref[1]
     chips, rows, _ = mine_ref.shape
     for chip in range(chips):
@@ -114,25 +105,21 @@
 
     zero_ref[...] = block(0)
     far_ref[...] = block(8)
-    for k, offset in enumerate((1, 3, 5, 7)):
-        odd_ref[k] = block(offset)
-        give_odd_ref[k] = block(-offset)
-    for k, offset in enumerate((2, 4, 6)):
-        even_ref[k] = block(offset)
-        give_even_ref[k] = block(-offset)
+    for k in range(7):
+        ahead_ref[k] = block(k + 1)
+        give_ref[k] = block(-(k + 1))
 
 
 def hidden_partial(place, mine, other, weight):
     units, depth = weight.shape
     tokens = mine.shape[0] * mine.shape[1] * 2
     width = tokens // Z
-    shapes = [(tokens, depth), (units, width), (units, width)]
-    shapes += [(count, units, width) for count in (4, 3, 4, 3)]
+    shapes = [(tokens, depth)] + [(units, width)] * 2 + [(7, units, width)] * 2
     return pl.pallas_call(
         hidden_partial_body,
         out_shape=[jax.ShapeDtypeStruct(shape, BF16) for shape in shapes],
         in_specs=[SMEM] + [VMEM] * 3,
-        out_specs=[VMEM] * 7,
+        out_specs=[VMEM] * 5,
         scratch_shapes=[pltpu.VMEM((units, tokens), BF16)],
         compiler_params=params(),
         cost_estimate=pl.CostEstimate(
@@ -144,9 +131,7 @@
     )(place, mine, other, weight)
 
 
-def down_body(acts_ref, cot_ref, weight_ref, m_ref, v_ref, *refs):
-    swish_ref, slope_ref, new_m_ref, new_v_ref, update_ref, sums_ref = refs[:6]
-    hidden, product = refs[6:]
+def activations_body(acts_ref, swish_ref, slope_ref, hidden_ref):
     blocks, units, width = acts_ref.shape
     units = units // 2
     chunk = 64
@@ -162,12 +147,34 @@
             s = jax.nn.sigmoid(g)
             swish = g * s
             slope = u * s * (1.0 + g * (1.0 - s))
-            hidden[rows, cols] = (swish * u).astype(BF16)
+            hidden_ref[rows, cols] = (swish * u).astype(BF16)
             swish_ref[rows, cols] = swish.astype(BF16)
             slope_ref[rows, cols] = slope.astype(BF16)
 
+
+def activations(acts):
+    blocks, units, width = acts.shape
+    units, tokens = units // 2, blocks * width
+    return pl.pallas_call(
+        activations_body,
+        out_shape=[jax.ShapeDtypeStruct((units, tokens), BF16)] * 3,
+        in_specs=[VMEM],
+        out_specs=[VMEM] * 3,
+        compiler_params=params(),
+        cost_estimate=pl.CostEstimate(
+            flops=30 * units * tokens,
+            bytes_accessed=10 * units * tokens,
+            transcendentals=units * tokens,
+        ),
+        name="activations",
+    )(acts)
+
+
+def down_body(hidden_ref, cot_ref, weight_ref, m_ref, v_ref, *refs):
+    new_m_ref, new_v_ref, update_ref, sums_ref, product = refs
+    units = weight_ref.shape[0]
     product[...] = lax.dot_general(
-        hidden[...], cot_ref[...], (((1,), (0,)), ((), ())), preferred_element_type=F32
+        hidden_ref[...], cot_ref[...], (((1,), (0,)), ((), ())), preferred_element_type=F32
     )
     step = 16
     depth = product.shape[1]
@@ -212,12 +219,10 @@
     return jnp.sum(first, axis=1, keepdims=True), jnp.sum(second, axis=1, keepdims=True)
 
 
-def down_update(acts, cotangent, weight, moment_m, moment_v):
-    units = acts.shape[1] // 2
-    tokens, depth = cotangent.shape
+def down_update(hidden, cotangent, weight, moment_m, moment_v):
+    units, tokens = hidden.shape
+    depth = cotangent.shape[1]
     shapes = [
-        jax.ShapeDtypeStruct((units, tokens), BF16),
-        jax.ShapeDtypeStruct((units, tokens), BF16),
         jax.ShapeDtypeStruct((units, depth), BF16),
         jax.ShapeDtypeStruct((units, depth), BF16),
         jax.ShapeDtypeStruct((units, depth), F32),
@@ -227,16 +232,16 @@
         down_body,
         out_shape=shapes,
         in_specs=[VMEM] * 5,
-        out_specs=[VMEM] * 6,
-        scratch_shapes=[pltpu.VMEM((units, tokens), BF16), pltpu.VMEM((units, depth), F32)],
-        compiler_params=params(),
-        cost_estimate=pl.CostEstimate(
-            flops=2 * units * depth * tokens + 30 * units * tokens,
-            bytes_accessed=8 * units * tokens + 2 * tokens * depth + 14 * units * depth,
-            transcendentals=units * tokens,
+        out_specs=[VMEM] * 4,
+        scratch_shapes=[pltpu.VMEM((units, depth), F32)],
+        compiler_params=params(),
+        cost_estimate=pl.CostEstimate(
+            flops=2 * units * depth * tokens,
+            bytes_accessed=2 * units * tokens + 2 * tokens * depth + 14 * units * depth,
+            transcendentals=0,
         ),
         name="down_update",
-    )(acts, cotangent, weight, moment_m, moment_v)
+    )(hidden, cotangent, weight, moment_m, moment_v)
 
 
 def group_body(number, count, place_ref, *refs):
@@ -467,17 +472,18 @@
     acts = jnp.concatenate([gate_pre.T, up_act.T], axis=0)
     acts, cotangent = lax.optimization_barrier((acts, cotangent))
     acts = lax.all_gather(acts, "row", axis=0, tiled=False)
-    cot_mine, cot_other = gather_chips(cotangent)
-    cotangent_all, zero, far, odd, even, give_odd, give_even = hidden_partial(
+    cot_mine = exchange_chips(jnp.broadcast_to(cotangent[None], (CHIPS, *cotangent.shape)))
+    cot_other = swap_core(cot_mine)
+    cotangent_all, zero, far, ahead, give = hidden_partial(
         place, cot_mine, cot_other, down_weight
     )
     tokens, _ = lax.optimization_barrier((tokens, cot_other))
-    tok_mine, tok_other = gather_chips(tokens)
-    swish, slope, new_m, new_v, update, sums = down_update(
-        acts, cotangent_all, down_weight, moment_m, moment_v
-    )
-    own, other = reduce_z(zero, far, odd, even, give_odd, give_even, sums)
-    own, tok_other = lax.optimization_barrier((own, tok_other))
+    tok_mine = exchange_chips(jnp.broadcast_to(tokens[None], (CHIPS, *tokens.shape)))
+    swish, slope, hidden = activations(acts)
+    new_m, new_v, update, sums = down_update(
+        hidden, cotangent_all, down_weight, moment_m, moment_v
+    )
+    own, other, (swish, tok_mine) = reduce_z(zero, far, ahead, give, (swish, tok_mine), sums)
 
     gate_weight, up_weight = gate_weight.T, up_weight.T
 
@@ -497,8 +503,9 @@
     ahead_even = swap_core(even_other[1:])
     group_0 = group(0, (even,))
     group_1 = group(1, (ahead_even,), group_0[4], group_0[3])
-    odd_other, odd, far, group_0, group_1 = lax.optimization_barrier(
-        (odd_other, odd, far, group_0, group_1)
+    tok_other = swap_core(tok_mine)
+    odd_other, odd, far, group_0, group_1, tok_other = lax.optimization_barrier(
+        (odd_other, odd, far, group_0, group_1, tok_other)
     )
     ahead_odd = swap_core(odd_other)
     group_2 = group(2, (odd,), group_1[4], group_1[3])

time: 241 us -> 248 us (1.029)
  starting transfers between devices: 116 us -> 132 us
  waiting for transfers between devices: 24.7 us -> 11.1 us
  local copies, waits for them, and re-layouts: 23 us -> 29.4 us
    ppermute x18 -> x24, starting transfers between devices: 74.3 us -> 93.5 us  [shift_z(): return lax.ppermute(v, ('row', 'col'), pairs)]
    ppermute x18 -> x24, waiting for transfers between devices: 15.7 us -> 3.18 us  [shift_z(): return lax.ppermute(v, ('row', 'col'), pairs)]
    unnamed x56 -> x72, local copies, waits for them, and re-layouts: 20.1 us -> 26.4 us
    ppermute x10 -> x9, starting transfers between devices: 34.1 us -> 30.4 us  [swap_core(): return lax.ppermute(v, 'col', [(c, c ^ 1) for c in range(COLS)])]
    pallas_call x0 -> x1, Pallas kernels: none -> 2.82 us  [activations(): pl.pallas_call(activations_body, out_shape=[jax.ShapeDtypeStruct((units,...]
    pallas_call x1, Pallas kernels: 6 us -> 3.21 us  [down_update(): pl.pallas_call(down_body, out_shape=shapes, in_specs=[VMEM] * 5, out_spec...]
    convert_element_type x10 -> x16, other arithmetic: 9.53 us -> 9.18 us  [add(): return total.astype(BF16)]
  transfers between devices with their start and end apart: 31 -> 36, of which waited for: 8 -> 6; matrix products, arithmetic and copies ran while one was open for 5% -> 5% of each run, Pallas kernels for 9% -> 8%
where the time goes in v1:
time: 248 us; the launch traced here: 246 us
  starting transfers between devices  132 us (53%)
  local copies, waits for them, and re-layouts  29.4 us (12%)
  Pallas kernels  23.9 us (10%)
  blocking collectives  23 us (9%)
  between operations  14.9 us (6%)
  other arithmetic  11.1 us (4%)
  waiting for transfers between devices  11.1 us (4%)
    ppermute x24, starting transfers between devices, shift_z(): return lax.ppermute(v, ('row', 'col'), pairs)  93.5 us
    ppermute x9, starting transfers between devices, swap_core(): return lax.ppermute(v, 'col', [(c, c ^ 1) for c in range(COLS)])  30.4 us
    unnamed x72, local copies, waits for them, and re-layouts  26.4 us
    all_to_all x1, blocking collectives, exchange_chips(): return lax.all_to_all(v, 'col', 0, 0, axis_index_groups=groups, tiled=True)  23 us
    convert_element_type x16, other arithmetic, add(): return total.astype(BF16)  9.18 us
    all_to_all x2, starting transfers between devices, exchange_chips(): return lax.all_to_all(v, 'col', 0, 0, axis_index_groups=groups, tiled=True)  8.44 us
    pallas_call x4, Pallas kernels, input_group(): pl.pallas_call(functools.partial(group_body, number, len(grads)), out_sha...  7.08 us
  transfers between devices with their start and end apart: 36, of which 6 were waited for; matrix products, arithmetic and copies ran while one was open for 5% of the time, Pallas kernels for 8%

profile of v1, /device:TPU:1, one launch (start us, length us, event | category | flops | bytes accessed | tf_op | source)
XLA Modules:
  0.0 245.6 jit_solution(15704427959756660433)
XLA Ops:
  7.2 1.7 pad_maximum_fusion.3
  9.9 23.0 %all_to_all.15.mine_ref = bf16[16,64,512]{2,1,0:T(8,128)(2,1)S(1)} all-to-all(bf16[16,64,512]{2,1,0:T(8,128)(2,1)S(1)} %broadcast_in_dim.4), channel_id=1, replica_groups={{0,2,4,6,8,10,12,14,16,18,20,22,24,26,28,30},{1,3,5,7,9,11,13,15,17,19,..., dimensions={0} | all-to-all | bytes 2097152 | tf_op jit(solution)/shard_map/all_to_all | solution.py:43
  32.9 4.8 %collective-permute-start = (bf16[16,64,512]{2,1,0:T(8,128)(2,1)S(1)}, bf16[16,64,512]{2,1,0:T(8,128)(2,1)S(1)}, u32[]{:S(2)}, u32[]{:S(2)}) collective-permute-start(bf16[16,64,512]{2,1,0:T(8,128)(2,1)S(1)} %all_to_all.15.mine_ref), channel_id=1, source_target_pairs={{0,1},{1,0},{2,3},{3,2},{4,5},{5,4},{6,7},{7,6},{8,9},{9,8},{10,11... | collective-permute-start | bytes 3145736 | tf_op jit(solution)/shard_map/ppermute | solution.py:38
  37.8 2.2 collective-permute-done.other_ref
  41.0 1.2 copy-done.18
  42.2 2.3 hidden_partial.1
  44.5 1.4 copy-done.5
  45.9 2.3 collective-permute-start.7
  48.2 10.8 %collective-permute-start.1 = (bf16[448,128]{1,0:T(8,128)(2,1)S(1)}, bf16[448,128]{1,0:T(8,128)(2,1)S(1)}, u32[]{:S(2)}, u32[]{:S(2)}) collective-permute-start(bf16[448,128]{1,0:T(8,128)(2,1)S(1)} %get-tuple-element.72), channel_id=1, source_target_pairs={{0,32},{1,481},{2,34},{3,483},{4,36},{5,485},{6,38},{7,487},{8,40}... | collective-permute-start | bytes 344072 | tf_op jit(solution)/shard_map/ppermute | solution.py:34
  59.0 1.1 broadcast_in_dim.5
  60.1 3.7 %all-to-all-start.1 = ((bf16[16,64,512]{2,1,0:T(8,128)(2,1)}), bf16[16,64,512]{2,1,0:T(8,128)(2,1)S(1)}, u32[]{:S(2)}, u32[]{:S(2)}) async-start(bf16[16,64,512]{2,1,0:T(8,128)(2,1)} %broadcast_in_dim.5), calls=%async_computation.1 | async-start | bytes 2097152 | tf_op jit(solution)/shard_map/all_to_all | solution.py:43
  63.8 4.1 %collective-permute-start.2 = (bf16[448,128]{1,0:T(8,128)(2,1)S(1)}, bf16[448,128]{1,0:T(8,128)(2,1)S(1)}, u32[]{:S(2)}, u32[]{:S(2)}) collective-permute-start(bf16[448,128]{1,0:T(8,128)(2,1)S(1)} %fusion.12), channel_id=1, source_target_pairs={{0,32},{1,481},{2,34},{3,483},{4,36},{5,485},{6,38},{7,487},{8,40}... | collective-permute-start | bytes 344072 | tf_op jit(solution)/shard_map/ppermute | solution.py:34
  68.8 1.9 collective-permute-start.8
  70.8 1.2 collective-permute-done.2
  72.0 5.3 %collective-permute-start.3 = (bf16[448,128]{1,0:T(8,128)(2,1)S(1)}, bf16[448,128]{1,0:T(8,128)(2,1)S(1)}, u32[]{:S(2)}, u32[]{:S(2)}) collective-permute-start(bf16[448,128]{1,0:T(8,128)(2,1)S(1)} %fusion.11), channel_id=1, source_target_pairs={{0,32},{1,481},{2,34},{3,483},{4,36},{5,485},{6,38},{7,487},{8,40}... | collective-permute-start | bytes 344072 | tf_op jit(solution)/shard_map/ppermute | solution.py:34
  78.3 3.4 %collective-permute-start.9 = (bf16[448,128]{1,0:T(8,128)(2,1)S(1)}, bf16[448,128]{1,0:T(8,128)(2,1)S(1)}, u32[]{:S(2)}, u32[]{:S(2)}) collective-permute-start(bf16[448,128]{1,0:T(8,128)(2,1)S(1)} %fusion.7), channel_id=1, source_target_pairs={{0,32},{1,481},{2,34},{3,483},{4,36},{5,485},{6,38},{7,487},{8,40}... | collective-permute-start | bytes 344072 | tf_op jit(solution)/shard_map/ppermute | solution.py:34
  81.7 4.5 %collective-permute-start.4 = (bf16[448,128]{1,0:T(8,128)(2,1)S(1)}, bf16[448,128]{1,0:T(8,128)(2,1)S(1)}, u32[]{:S(2)}, u32[]{:S(2)}) collective-permute-start(bf16[448,128]{1,0:T(8,128)(2,1)S(1)} %fusion.10), channel_id=1, source_target_pairs={{0,32},{1,481},{2,34},{3,483},{4,36},{5,485},{6,38},{7,487},{8,40}... | collective-permute-start | bytes 344072 | tf_op jit(solution)/shard_map/ppermute | solution.py:34
  87.2 4.6 %collective-permute-start.10 = (bf16[448,128]{1,0:T(8,128)(2,1)S(1)}, bf16[448,128]{1,0:T(8,128)(2,1)S(1)}, u32[]{:S(2)}, u32[]{:S(2)}) collective-permute-start(bf16[448,128]{1,0:T(8,128)(2,1)S(1)} %fusion.6), channel_id=1, source_target_pairs={{0,32},{1,481},{2,34},{3,483},{4,36},{5,485},{6,38},{7,487},{8,40}... | collective-permute-start | bytes 344072 | tf_op jit(solution)/shard_map/ppermute | solution.py:34
  91.8 2.2 collective-permute-start.5
  95.0 5.3 %collective-permute-start.11 = (bf16[448,128]{1,0:T(8,128)(2,1)S(1)}, bf16[448,128]{1,0:T(8,128)(2,1)S(1)}, u32[]{:S(2)}, u32[]{:S(2)}) collective-permute-start(bf16[448,128]{1,0:T(8,128)(2,1)S(1)} %fusion.5), channel_id=1, source_target_pairs={{0,32},{1,481},{2,34},{3,483},{4,36},{5,485},{6,38},{7,487},{8,40}... | collective-permute-start | bytes 344072 | tf_op jit(solution)/shard_map/ppermute | solution.py:34
  101.0 1.9 collective-permute-start.6
  102.9 1.6 fusion.4
  104.5 4.1 %collective-permute-start.12 = (bf16[448,128]{1,0:T(8,128)(2,1)}, bf16[448,128]{1,0:T(8,128)(2,1)}, u32[]{:S(2)}, u32[]{:S(2)}) collective-permute-start(bf16[448,128]{1,0:T(8,128)(2,1)} %fusion.4), channel_id=1, source_target_pairs={{0,32},{1,481},{2,34},{3,483},{4,36},{5,485},{6,38},{7,487},{8,40}... | collective-permute-start | bytes 344072 | tf_op jit(solution)/shard_map/ppermute | solution.py:34
  108.7 2.0 copy-done.4
  110.7 2.8 %activations.1 = (bf16[448,2048]{1,0:T(8,128)(2,1)S(1)}, bf16[448,2048]{1,0:T(8,128)(2,1)S(1)}, bf16[448,2048]{1,0:T(8,128)(2,1)S(1)}) custom-call(bf16[16,896,128]{2,1,0:T(8,128)(2,1)S(1)} %bitcast.81), custom_call_target="tpu_custom_call" | custom-call | flops 27525120 | bytes 9175040 | tf_op jit(solution)/shard_map/activations/pallas_call | solution.py:158
  113.5 1.2 copy-done
  114.8 1.2 copy-done.7
  117.0 1.9 collective-permute-start.15
  119.9 2.8 %collective-permute-start.13 = (bf16[448,128]{1,0:T(8,128)(2,1)S(1)}, bf16[448,128]{1,0:T(8,128)(2,1)S(1)}, u32[]{:S(2)}, u32[]{:S(2)}) collective-permute-start(bf16[448,128]{1,0:T(8,128)(2,1)S(1)} %fusion.3), channel_id=1, source_target_pairs={{0,32},{1,481},{2,34},{3,483},{4,36},{5,485},{6,38},{7,487},{8,40}... | collective-permute-start | bytes 344072 | tf_op jit(solution)/shard_map/ppermute | solution.py:34
  123.7 2.9 %collective-permute-start.16 = (bf16[448,128]{1,0:T(8,128)(2,1)S(1)}, bf16[448,128]{1,0:T(8,128)(2,1)S(1)}, u32[]{:S(2)}, u32[]{:S(2)}) collective-permute-start(bf16[448,128]{1,0:T(8,128)(2,1)S(1)} %fusion), channel_id=1, source_target_pairs={{0,32},{1,481},{2,34},{3,483},{4,36},{5,485},{6,38},{7,487},{8,40}... | collective-permute-start | bytes 344072 | tf_op jit(solution)/shard_map/ppermute | solution.py:34
  127.6 3.1 %collective-permute-start.14 = (bf16[448,128]{1,0:T(8,128)(2,1)S(1)}, bf16[448,128]{1,0:T(8,128)(2,1)S(1)}, u32[]{:S(2)}, u32[]{:S(2)}) collective-permute-start(bf16[448,128]{1,0:T(8,128)(2,1)S(1)} %fusion.2), channel_id=1, source_target_pairs={{0,32},{1,481},{2,34},{3,483},{4,36},{5,485},{6,38},{7,487},{8,40}... | collective-permute-start | bytes 344072 | tf_op jit(solution)/shard_map/ppermute | solution.py:34
  130.7 1.6 copy-done.6
  132.3 1.5 copy-done.8
  135.8 3.2 %down_update.1 = (bf16[448,512]{1,0:T(8,128)(2,1)}, bf16[448,512]{1,0:T(8,128)(2,1)}, f32[448,512]{1,0:T(8,128)S(1)}, bf16[16,128]{1,0:T(8,128)(2,1)S(1)}) custom-call(bf16[448,2048]{1,0:T(8,128)(2,1)S(1)} %copy-done.8, bf16[2048,512]{1,0:T(8,128)(2,1)S(1)} %copy-done.6, bf16[448,512]{1,0:T(8,128)(2,1)S(1)} %copy-done.12, bf16[448,512]{1,0:T(8,128)(2,1)S(1)} %copy-done.13, ...), custom_call_target="tpu_custom_call" | custom-call | flops 939524096 | bytes 7143424 | tf_op jit(solution)/shard_map/down_update/pallas_call | solution.py:231
  139.1 4.8 %collective-permute-start.17 = (bf16[464,128]{1,0:T(8,128)(2,1)S(1)}, bf16[464,128]{1,0:T(8,128)(2,1)S(1)}, u32[]{:S(2)}, u32[]{:S(2)}) collective-permute-start(bf16[464,128]{1,0:T(8,128)(2,1)S(1)} %pad_maximum_fusion.4), channel_id=1, source_target_pairs={{0,1},{1,0},{2,3},{3,2},{4,5},{5,4},{6,7},{7,6},{8,9},{9,8},{10,11... | collective-permute-start | bytes 356360 | tf_op jit(solution)/shard_map/ppermute | solution.py:38
  144.0 1.9 collective-permute-start.29
  145.9 2.4 collective-permute-start.22
  148.4 4.6 %collective-permute-start.18 = (bf16[464,128]{1,0:T(8,128)(2,1)S(1)}, bf16[464,128]{1,0:T(8,128)(2,1)S(1)}, u32[]{:S(2)}, u32[]{:S(2)}) collective-permute-start(bf16[464,128]{1,0:T(8,128)(2,1)S(1)} %add_convert_fusion.1), channel_id=1, source_target_pairs={{0,64},{1,449},{2,66},{3,451},{4,68},{5,453},{6,70},{7,455},{8,72}... | collective-permute-start | bytes 356360 | tf_op jit(solution)/shard_map/ppermute | solution.py:34
  153.0 2.1 collective-permute-start.23
  155.1 1.4 collective-permute-done.18
  156.4 5.4 %collective-permute-start.19 = (bf16[464,128]{1,0:T(8,128)(2,1)S(1)}, bf16[464,128]{1,0:T(8,128)(2,1)S(1)}, u32[]{:S(2)}, u32[]{:S(2)}) collective-permute-start(bf16[464,128]{1,0:T(8,128)(2,1)S(1)} %collective-permute-done.18), channel_id=1, source_target_pairs={{0,64},{1,449},{2,66},{3,451},{4,68},{5,453},{6,70},{7,455},{8,72}... | collective-permute-start | bytes 356360 | tf_op jit(solution)/shard_map/ppermute | solution.py:34
  161.9 2.5 %collective-permute-start.24 = (bf16[464,128]{1,0:T(8,128)(2,1)S(1)}, bf16[464,128]{1,0:T(8,128)(2,1)S(1)}, u32[]{:S(2)}, u32[]{:S(2)}) collective-permute-start(bf16[464,128]{1,0:T(8,128)(2,1)S(1)} %collective-permute-done.23), channel_id=1, source_target_pairs={{0,64},{1,449},{2,66},{3,451},{4,68},{5,453},{6,70},{7,455},{8,72}... | collective-permute-start | bytes 356360 | tf_op jit(solution)/shard_map/ppermute | solution.py:34
  164.4 6.0 %collective-permute-start.20 = (bf16[464,128]{1,0:T(8,128)(2,1)S(1)}, bf16[464,128]{1,0:T(8,128)(2,1)S(1)}, u32[]{:S(2)}, u32[]{:S(2)}) collective-permute-start(bf16[464,128]{1,0:T(8,128)(2,1)S(1)} %collective-permute-done.19), channel_id=1, source_target_pairs={{0,64},{1,449},{2,66},{3,451},{4,68},{5,453},{6,70},{7,455},{8,72}... | collective-permute-start | bytes 356360 | tf_op jit(solution)/shard_map/ppermute | solution.py:34
  170.4 2.7 %collective-permute-start.25 = (bf16[464,128]{1,0:T(8,128)(2,1)S(1)}, bf16[464,128]{1,0:T(8,128)(2,1)S(1)}, u32[]{:S(2)}, u32[]{:S(2)}) collective-permute-start(bf16[464,128]{1,0:T(8,128)(2,1)S(1)} %collective-permute-done.24), channel_id=1, source_target_pairs={{0,64},{1,449},{2,66},{3,451},{4,68},{5,453},{6,70},{7,455},{8,72}... | collective-permute-start | bytes 356360 | tf_op jit(solution)/shard_map/ppermute | solution.py:34
  173.2 3.5 %collective-permute-start.21 = (bf16[4,464,128]{2,1,0:T(8,128)(2,1)S(1)}, bf16[4,464,128]{2,1,0:T(8,128)(2,1)S(1)}, u32[]{:S(2)}, u32[]{:S(2)}) collective-permute-start(bf16[4,464,128]{2,1,0:T(8,128)(2,1)S(1)} %pad_maximum_fusion), channel_id=1, source_target_pairs={{0,32},{1,481},{2,34},{3,483},{4,36},{5,485},{6,38},{7,487},{8,40}... | collective-permute-start | bytes 1425416 | tf_op jit(solution)/shard_map/ppermute | solution.py:34
  177.3 3.5 %collective-permute-start.26 = (bf16[4,464,128]{2,1,0:T(8,128)(2,1)S(1)}, bf16[4,464,128]{2,1,0:T(8,128)(2,1)S(1)}, u32[]{:S(2)}, u32[]{:S(2)}) collective-permute-start(bf16[4,464,128]{2,1,0:T(8,128)(2,1)S(1)} %pad_maximum_fusion.1.refs_0_), channel_id=1, source_target_pairs={{0,32},{1,481},{2,34},{3,483},{4,36},{5,485},{6,38},{7,487},{8,40}... | collective-permute-start | bytes 1425416 | tf_op jit(solution)/shard_map/ppermute | solution.py:34
  180.9 7.0 %collective-permute-start.28 = (bf16[3,464,128]{2,1,0:T(8,128)(2,1)S(1)}, bf16[3,464,128]{2,1,0:T(8,128)(2,1)S(1)}, u32[]{:S(2)}, u32[]{:S(2)}) collective-permute-start(bf16[3,464,128]{2,1,0:T(8,128)(2,1)S(1)} %pad_maximum_fusion.2), channel_id=1, source_target_pairs={{0,1},{1,0},{2,3},{3,2},{4,5},{5,4},{6,7},{7,6},{8,9},{9,8},{10,11... | collective-permute-start | bytes 1069064 | tf_op jit(solution)/shard_map/ppermute | solution.py:38
  187.8 4.3 %collective-permute-start.27 = (bf16[464,128]{1,0:T(8,128)(2,1)S(1)}, bf16[464,128]{1,0:T(8,128)(2,1)S(1)}, u32[]{:S(2)}, u32[]{:S(2)}) collective-permute-start(bf16[464,128]{1,0:T(8,128)(2,1)S(1)} %collective-permute-done.25), channel_id=1, source_target_pairs={{0,64},{1,449},{2,66},{3,451},{4,68},{5,453},{6,70},{7,455},{8,72}... | collective-permute-start | bytes 356360 | tf_op jit(solution)/shard_map/ppermute | solution.py:34
  192.2 1.8 input_group.4
  194.7 1.5 input_group.5
  197.1 2.9 %collective-permute-start.30 = (bf16[4,464,128]{2,1,0:T(8,128)(2,1)S(1)}, bf16[4,464,128]{2,1,0:T(8,128)(2,1)S(1)}, u32[]{:S(2)}, u32[]{:S(2)}) collective-permute-start(bf16[4,464,128]{2,1,0:T(8,128)(2,1)S(1)} %collective-permute-done.21), channel_id=1, source_target_pairs={{0,1},{1,0},{2,3},{3,2},{4,5},{5,4},{6,7},{7,6},{8,9},{9,8},{10,11... | collective-permute-start | bytes 1425416 | tf_op jit(solution)/shard_map/ppermute | solution.py:38
  200.0 1.8 input_group.6
  202.6 1.9 collective-permute-start.31
  204.5 2.0 input_group.7
  208.1 2.4 collective-permute-start.32
  210.5 1.2 collective-permute-done.32.refs_5_
  211.8 2.0 merge_cores.1
  213.8 4.8 %all-to-all-start.2 = ((bf16[16,272,128]{2,1,0:T(8,128)(2,1)}), bf16[16,272,128]{2,1,0:T(8,128)(2,1)S(1)}, u32[]{:S(2)}, u32[]{:S(2)}) async-start(bf16[16,272,128]{2,1,0:T(8,128)(2,1)} %merge_cores.1), calls=%async_computation.2 | async-start | bytes 2228224 | tf_op jit(solution)/shard_map/all_to_all | solution.py:43
  218.6 1.1 copy-done.20
  219.7 1.1 copy-done.22
  226.8 4.5 %weight_grads.1 = (bf16[448,512]{1,0:T(8,128)(2,1)}, bf16[448,512]{1,0:T(8,128)(2,1)}) custom-call(s32[3]{0:T(128)S(1)} %pad_add_fusion.place_ref, bf16[448,512]{1,0:T(8,128)(2,1)S(1)} %copy-done.24, bf16[448,384]{1,0:T(8,128)(2,1)S(1)} %copy-done.32, bf16[448,512]{1,0:T(8,128)(2,1)S(1)} %copy-done.28, bf16[448,640]{1,0:T(8,128)(2,1)S(1)} %copy-done.20, ...), custom_call_target="tpu_custom_call" | custom-call | flops 1879048192 | bytes 6684672 | tf_op jit(solution)/shard_map/weight_grads/pallas_call | solution.py:449
  231.3 4.4 %all-to-all-done.2.arrived_ref = bf16[16,272,128]{2,1,0:T(8,128)(2,1)S(1)} async-done(((bf16[16,272,128]{2,1,0:T(8,128)(2,1)}), bf16[16,272,128]{2,1,0:T(8,128)(2,1)S(1)}, u32[]{:S(2)}, u32[]{:S(2)}) %all-to-all-start.2) | async-done | bytes 1114144 | tf_op jit(solution)/shard_map/all_to_all | solution.py:43
  235.6 1.2 copy-done.10
  236.8 2.0 finish.1
  (118 shorter events, 23.5 us)
Async XLA Ops:
  7.2 101.5 %all-gather.3.cloned.1.call-start = ((), (), s32[]{:S(2)}) async-start(), calls=%async_computation.3 | async-start | bytes 3899392 | tf_op jit(solution)/shard_map/all_gather | solution.py:474
  8.9 32.1 %copy-start.12 = (bf16[448,512]{1,0:T(8,128)(2,1)S(1)}, bf16[448,512]{1,0:T(8,128)(2,1)}, u32[]{:S(2)}) copy-start(bf16[448,512]{1,0:T(8,128)(2,1)} %weight_ref.3) | copy-start | bytes 1376260
  9.9 49.1 %copy-start.35 = (bf16[64,512]{1,0:T(8,128)(2,1)S(1)}, bf16[64,512]{1,0:T(8,128)(2,1)}, u32[]{:S(2)}) copy-start(bf16[64,512]{1,0:T(8,128)(2,1)} %param.9) | copy-start | bytes 196612
  32.9 7.1 %collective-permute-start = (bf16[16,64,512]{2,1,0:T(8,128)(2,1)S(1)}, bf16[16,64,512]{2,1,0:T(8,128)(2,1)S(1)}, u32[]{:S(2)}, u32[]{:S(2)}) collective-permute-start(bf16[16,64,512]{2,1,0:T(8,128)(2,1)S(1)} %all_to_all.15.mine_ref), channel_id=1, source_target_pairs={{0,1},{1,0},{2,3},{3,2},{4,5},{5,4},{6,7},{7,6},{8,9},{9,8},{10,11... | collective-permute-start | bytes 3145736 | tf_op jit(solution)/shard_map/ppermute | solution.py:38
  41.0 1.2 copy-start.18
  44.5 1.4 copy-start.5
  45.9 54.4 %copy-start.11 = (bf16[7,448,128]{2,1,0:T(8,128)(2,1)}, bf16[7,448,128]{2,1,0:T(8,128)(2,1)S(1)}, u32[]{:S(2)}) copy-start(bf16[7,448,128]{2,1,0:T(8,128)(2,1)S(1)} %get-tuple-element.73) | copy-start | bytes 2408452
  45.9 22.0 %collective-permute-start.7 = (bf16[7,448,128]{2,1,0:T(8,128)(2,1)S(1)}, bf16[7,448,128]{2,1,0:T(8,128)(2,1)}, u32[]{:S(2)}, u32[]{:S(2)}) collective-permute-start(bf16[7,448,128]{2,1,0:T(8,128)(2,1)S(1)} %get-tuple-element.74), channel_id=1, source_target_pairs={{0,1},{1,0},{2,3},{3,2},{4,5},{5,4},{6,7},{7,6},{8,9},{9,8},{10,11... | collective-permute-start | bytes 2408456 | tf_op jit(solution)/shard_map/ppermute | solution.py:38
  48.2 15.6 %collective-permute-start.1 = (bf16[448,128]{1,0:T(8,128)(2,1)S(1)}, bf16[448,128]{1,0:T(8,128)(2,1)S(1)}, u32[]{:S(2)}, u32[]{:S(2)}) collective-permute-start(bf16[448,128]{1,0:T(8,128)(2,1)S(1)} %get-tuple-element.72), channel_id=1, source_target_pairs={{0,32},{1,481},{2,34},{3,483},{4,36},{5,485},{6,38},{7,487},{8,40}... | collective-permute-start | bytes 344072 | tf_op jit(solution)/shard_map/ppermute | solution.py:34
  60.1 55.9 %all-to-all-start.1 = ((bf16[16,64,512]{2,1,0:T(8,128)(2,1)}), bf16[16,64,512]{2,1,0:T(8,128)(2,1)S(1)}, u32[]{:S(2)}, u32[]{:S(2)}) async-start(bf16[16,64,512]{2,1,0:T(8,128)(2,1)} %broadcast_in_dim.5), calls=%async_computation.1 | async-start | bytes 2097152 | tf_op jit(solution)/shard_map/all_to_all | solution.py:43
  63.8 8.1 %collective-permute-start.2 = (bf16[448,128]{1,0:T(8,128)(2,1)S(1)}, bf16[448,128]{1,0:T(8,128)(2,1)S(1)}, u32[]{:S(2)}, u32[]{:S(2)}) collective-permute-start(bf16[448,128]{1,0:T(8,128)(2,1)S(1)} %fusion.12), channel_id=1, source_target_pairs={{0,32},{1,481},{2,34},{3,483},{4,36},{5,485},{6,38},{7,487},{8,40}... | collective-permute-start | bytes 344072 | tf_op jit(solution)/shard_map/ppermute | solution.py:34
  68.8 8.5 %collective-permute-start.8 = (bf16[448,128]{1,0:T(8,128)(2,1)S(1)}, bf16[448,128]{1,0:T(8,128)(2,1)S(1)}, u32[]{:S(2)}, u32[]{:S(2)}) collective-permute-start(bf16[448,128]{1,0:T(8,128)(2,1)S(1)} %slice_bitcast_fusion.6), channel_id=1, source_target_pairs={{0,32},{1,481},{2,34},{3,483},{4,36},{5,485},{6,38},{7,487},{8,40}... | collective-permute-start | bytes 344072 | tf_op jit(solution)/shard_map/ppermute | solution.py:34
  72.0 9.7 %collective-permute-start.3 = (bf16[448,128]{1,0:T(8,128)(2,1)S(1)}, bf16[448,128]{1,0:T(8,128)(2,1)S(1)}, u32[]{:S(2)}, u32[]{:S(2)}) collective-permute-start(bf16[448,128]{1,0:T(8,128)(2,1)S(1)} %fusion.11), channel_id=1, source_target_pairs={{0,32},{1,481},{2,34},{3,483},{4,36},{5,485},{6,38},{7,487},{8,40}... | collective-permute-start | bytes 344072 | tf_op jit(solution)/shard_map/ppermute | solution.py:34
  78.3 7.9 %collective-permute-start.9 = (bf16[448,128]{1,0:T(8,128)(2,1)S(1)}, bf16[448,128]{1,0:T(8,128)(2,1)S(1)}, u32[]{:S(2)}, u32[]{:S(2)}) collective-permute-start(bf16[448,128]{1,0:T(8,128)(2,1)S(1)} %fusion.7), channel_id=1, source_target_pairs={{0,32},{1,481},{2,34},{3,483},{4,36},{5,485},{6,38},{7,487},{8,40}... | collective-permute-start | bytes 344072 | tf_op jit(solution)/shard_map/ppermute | solution.py:34
  81.7 10.1 %collective-permute-start.4 = (bf16[448,128]{1,0:T(8,128)(2,1)S(1)}, bf16[448,128]{1,0:T(8,128)(2,1)S(1)}, u32[]{:S(2)}, u32[]{:S(2)}) collective-permute-start(bf16[448,128]{1,0:T(8,128)(2,1)S(1)} %fusion.10), channel_id=1, source_target_pairs={{0,32},{1,481},{2,34},{3,483},{4,36},{5,485},{6,38},{7,487},{8,40}... | collective-permute-start | bytes 344072 | tf_op jit(solution)/shard_map/ppermute | solution.py:34
  87.2 6.9 %collective-permute-start.10 = (bf16[448,128]{1,0:T(8,128)(2,1)S(1)}, bf16[448,128]{1,0:T(8,128)(2,1)S(1)}, u32[]{:S(2)}, u32[]{:S(2)}) collective-permute-start(bf16[448,128]{1,0:T(8,128)(2,1)S(1)} %fusion.6), channel_id=1, source_target_pairs={{0,32},{1,481},{2,34},{3,483},{4,36},{5,485},{6,38},{7,487},{8,40}... | collective-permute-start | bytes 344072 | tf_op jit(solution)/shard_map/ppermute | solution.py:34
  91.8 8.5 %collective-permute-start.5 = (bf16[448,128]{1,0:T(8,128)(2,1)S(1)}, bf16[448,128]{1,0:T(8,128)(2,1)S(1)}, u32[]{:S(2)}, u32[]{:S(2)}) collective-permute-start(bf16[448,128]{1,0:T(8,128)(2,1)S(1)} %fusion.9), channel_id=1, source_target_pairs={{0,32},{1,481},{2,34},{3,483},{4,36},{5,485},{6,38},{7,487},{8,40}... | collective-permute-start | bytes 344072 | tf_op jit(solution)/shard_map/ppermute | solution.py:34
  95.0 7.9 %collective-permute-start.11 = (bf16[448,128]{1,0:T(8,128)(2,1)S(1)}, bf16[448,128]{1,0:T(8,128)(2,1)S(1)}, u32[]{:S(2)}, u32[]{:S(2)}) collective-permute-start(bf16[448,128]{1,0:T(8,128)(2,1)S(1)} %fusion.5), channel_id=1, source_target_pairs={{0,32},{1,481},{2,34},{3,483},{4,36},{5,485},{6,38},{7,487},{8,40}... | collective-permute-start | bytes 344072 | tf_op jit(solution)/shard_map/ppermute | solution.py:34
  101.0 15.0 %collective-permute-start.6 = (bf16[448,128]{1,0:T(8,128)(2,1)}, bf16[448,128]{1,0:T(8,128)(2,1)}, u32[]{:S(2)}, u32[]{:S(2)}) collective-permute-start(bf16[448,128]{1,0:T(8,128)(2,1)} %fusion.8), channel_id=1, source_target_pairs={{0,32},{1,481},{2,34},{3,483},{4,36},{5,485},{6,38},{7,487},{8,40}... | collective-permute-start | bytes 344072 | tf_op jit(solution)/shard_map/ppermute | solution.py:34
  104.5 11.5 %collective-permute-start.12 = (bf16[448,128]{1,0:T(8,128)(2,1)}, bf16[448,128]{1,0:T(8,128)(2,1)}, u32[]{:S(2)}, u32[]{:S(2)}) collective-permute-start(bf16[448,128]{1,0:T(8,128)(2,1)} %fusion.4), channel_id=1, source_target_pairs={{0,32},{1,481},{2,34},{3,483},{4,36},{5,485},{6,38},{7,487},{8,40}... | collective-permute-start | bytes 344072 | tf_op jit(solution)/shard_map/ppermute | solution.py:34
  108.7 2.0 copy-start.4
  113.5 1.2 copy-start
  114.8 1.2 copy-start.7
  117.0 5.8 %collective-permute-start.15 = (bf16[448,128]{1,0:T(8,128)(2,1)S(1)}, bf16[448,128]{1,0:T(8,128)(2,1)S(1)}, u32[]{:S(2)}, u32[]{:S(2)}) collective-permute-start(bf16[448,128]{1,0:T(8,128)(2,1)S(1)} %fusion.1), channel_id=1, source_target_pairs={{0,32},{1,481},{2,34},{3,483},{4,36},{5,485},{6,38},{7,487},{8,40}... | collective-permute-start | bytes 344072 | tf_op jit(solution)/shard_map/ppermute | solution.py:34
  119.9 6.7 %collective-permute-start.13 = (bf16[448,128]{1,0:T(8,128)(2,1)S(1)}, bf16[448,128]{1,0:T(8,128)(2,1)S(1)}, u32[]{:S(2)}, u32[]{:S(2)}) collective-permute-start(bf16[448,128]{1,0:T(8,128)(2,1)S(1)} %fusion.3), channel_id=1, source_target_pairs={{0,32},{1,481},{2,34},{3,483},{4,36},{5,485},{6,38},{7,487},{8,40}... | collective-permute-start | bytes 344072 | tf_op jit(solution)/shard_map/ppermute | solution.py:34
  123.7 15.3 %collective-permute-start.16 = (bf16[448,128]{1,0:T(8,128)(2,1)S(1)}, bf16[448,128]{1,0:T(8,128)(2,1)S(1)}, u32[]{:S(2)}, u32[]{:S(2)}) collective-permute-start(bf16[448,128]{1,0:T(8,128)(2,1)S(1)} %fusion), channel_id=1, source_target_pairs={{0,32},{1,481},{2,34},{3,483},{4,36},{5,485},{6,38},{7,487},{8,40}... | collective-permute-start | bytes 344072 | tf_op jit(solution)/shard_map/ppermute | solution.py:34
  127.6 11.5 %collective-permute-start.14 = (bf16[448,128]{1,0:T(8,128)(2,1)S(1)}, bf16[448,128]{1,0:T(8,128)(2,1)S(1)}, u32[]{:S(2)}, u32[]{:S(2)}) collective-permute-start(bf16[448,128]{1,0:T(8,128)(2,1)S(1)} %fusion.2), channel_id=1, source_target_pairs={{0,32},{1,481},{2,34},{3,483},{4,36},{5,485},{6,38},{7,487},{8,40}... | collective-permute-start | bytes 344072 | tf_op jit(solution)/shard_map/ppermute | solution.py:34
  130.7 1.6 copy-start.6
  132.3 1.5 copy-start.8
  133.8 1.0 copy-start.13
  134.8 1.0 copy-start.14
  139.0 41.8 %copy-start.9 = (f32[448,512]{1,0:T(8,128)}, f32[448,512]{1,0:T(8,128)S(1)}, u32[]{:S(2)}) copy-start(f32[448,512]{1,0:T(8,128)S(1)} %get-tuple-element.127.update_ref) | copy-start | bytes 2752516
  139.1 53.1 %copy-start.1 = (bf16[448,2048]{1,0:T(8,128)(2,1)S(1)}, bf16[448,2048]{1,0:T(8,128)(2,1)}, u32[]{:S(2)}) copy-start(bf16[448,2048]{1,0:T(8,128)(2,1)} %copy-done) | copy-start | bytes 5505028
  139.1 53.1 %copy-start.2 = (bf16[512,448]{0,1:T(8,128)(2,1)S(1)}, bf16[512,448]{0,1:T(8,128)(2,1)}, u32[]{:S(2)}) copy-start(bf16[512,448]{0,1:T(8,128)(2,1)} %param.13) | copy-start | bytes 1376260
  139.1 53.1 %copy-start.3 = (bf16[512,448]{0,1:T(8,128)(2,1)S(1)}, bf16[512,448]{0,1:T(8,128)(2,1)}, u32[]{:S(2)}) copy-start(bf16[512,448]{0,1:T(8,128)(2,1)} %param.14) | copy-start | bytes 1376260
  139.1 9.2 %collective-permute-start.17 = (bf16[464,128]{1,0:T(8,128)(2,1)S(1)}, bf16[464,128]{1,0:T(8,128)(2,1)S(1)}, u32[]{:S(2)}, u32[]{:S(2)}) collective-permute-start(bf16[464,128]{1,0:T(8,128)(2,1)S(1)} %pad_maximum_fusion.4), channel_id=1, source_target_pairs={{0,1},{1,0},{2,3},{3,2},{4,5},{5,4},{6,7},{7,6},{8,9},{9,8},{10,11... | collective-permute-start | bytes 356360 | tf_op jit(solution)/shard_map/ppermute | solution.py:38
  144.0 53.0 %collective-permute-start.29 = (bf16[16,64,512]{2,1,0:T(8,128)(2,1)S(1)}, bf16[16,64,512]{2,1,0:T(8,128)(2,1)S(1)}, u32[]{:S(2)}, u32[]{:S(2)}) collective-permute-start(bf16[16,64,512]{2,1,0:T(8,128)(2,1)S(1)} %all-to-all-done.1.refs_8_), channel_id=1, source_target_pairs={{0,1},{1,0},{2,3},{3,2},{4,5},{5,4},{6,7},{7,6},{8,9},{9,8},{10,11... | collective-permute-start | bytes 3145736 | tf_op jit(solution)/shard_map/ppermute | solution.py:38
  145.9 7.0 %collective-permute-start.22 = (bf16[464,128]{1,0:T(8,128)(2,1)S(1)}, bf16[464,128]{1,0:T(8,128)(2,1)S(1)}, u32[]{:S(2)}, u32[]{:S(2)}) collective-permute-start(bf16[464,128]{1,0:T(8,128)(2,1)S(1)} %concatenate.11), channel_id=1, source_target_pairs={{0,1},{1,0},{2,3},{3,2},{4,5},{5,4},{6,7},{7,6},{8,9},{9,8},{10,11... | collective-permute-start | bytes 356360 | tf_op jit(solution)/shard_map/ppermute | solution.py:38
  148.4 8.0 %collective-permute-start.18 = (bf16[464,128]{1,0:T(8,128)(2,1)S(1)}, bf16[464,128]{1,0:T(8,128)(2,1)S(1)}, u32[]{:S(2)}, u32[]{:S(2)}) collective-permute-start(bf16[464,128]{1,0:T(8,128)(2,1)S(1)} %add_convert_fusion.1), channel_id=1, source_target_pairs={{0,64},{1,449},{2,66},{3,451},{4,68},{5,453},{6,70},{7,455},{8,72}... | collective-permute-start | bytes 356360 | tf_op jit(solution)/shard_map/ppermute | solution.py:34
  153.0 8.9 %collective-permute-start.23 = (bf16[464,128]{1,0:T(8,128)(2,1)S(1)}, bf16[464,128]{1,0:T(8,128)(2,1)S(1)}, u32[]{:S(2)}, u32[]{:S(2)}) collective-permute-start(bf16[464,128]{1,0:T(8,128)(2,1)S(1)} %add_convert_fusion), channel_id=1, source_target_pairs={{0,64},{1,449},{2,66},{3,451},{4,68},{5,453},{6,70},{7,455},{8,72}... | collective-permute-start | bytes 356360 | tf_op jit(solution)/shard_map/ppermute | solution.py:34
  156.4 8.0 %collective-permute-start.19 = (bf16[464,128]{1,0:T(8,128)(2,1)S(1)}, bf16[464,128]{1,0:T(8,128)(2,1)S(1)}, u32[]{:S(2)}, u32[]{:S(2)}) collective-permute-start(bf16[464,128]{1,0:T(8,128)(2,1)S(1)} %collective-permute-done.18), channel_id=1, source_target_pairs={{0,64},{1,449},{2,66},{3,451},{4,68},{5,453},{6,70},{7,455},{8,72}... | collective-permute-start | bytes 356360 | tf_op jit(solution)/shard_map/ppermute | solution.py:34
  161.9 8.5 %collective-permute-start.24 = (bf16[464,128]{1,0:T(8,128)(2,1)S(1)}, bf16[464,128]{1,0:T(8,128)(2,1)S(1)}, u32[]{:S(2)}, u32[]{:S(2)}) collective-permute-start(bf16[464,128]{1,0:T(8,128)(2,1)S(1)} %collective-permute-done.23), channel_id=1, source_target_pairs={{0,64},{1,449},{2,66},{3,451},{4,68},{5,453},{6,70},{7,455},{8,72}... | collective-permute-start | bytes 356360 | tf_op jit(solution)/shard_map/ppermute | solution.py:34
  164.4 8.7 %collective-permute-start.20 = (bf16[464,128]{1,0:T(8,128)(2,1)S(1)}, bf16[464,128]{1,0:T(8,128)(2,1)S(1)}, u32[]{:S(2)}, u32[]{:S(2)}) collective-permute-start(bf16[464,128]{1,0:T(8,128)(2,1)S(1)} %collective-permute-done.19), channel_id=1, source_target_pairs={{0,64},{1,449},{2,66},{3,451},{4,68},{5,453},{6,70},{7,455},{8,72}... | collective-permute-start | bytes 356360 | tf_op jit(solution)/shard_map/ppermute | solution.py:34
  170.4 6.8 %collective-permute-start.25 = (bf16[464,128]{1,0:T(8,128)(2,1)S(1)}, bf16[464,128]{1,0:T(8,128)(2,1)S(1)}, u32[]{:S(2)}, u32[]{:S(2)}) collective-permute-start(bf16[464,128]{1,0:T(8,128)(2,1)S(1)} %collective-permute-done.24), channel_id=1, source_target_pairs={{0,64},{1,449},{2,66},{3,451},{4,68},{5,453},{6,70},{7,455},{8,72}... | collective-permute-start | bytes 356360 | tf_op jit(solution)/shard_map/ppermute | solution.py:34
  173.2 23.8 %collective-permute-start.21 = (bf16[4,464,128]{2,1,0:T(8,128)(2,1)S(1)}, bf16[4,464,128]{2,1,0:T(8,128)(2,1)S(1)}, u32[]{:S(2)}, u32[]{:S(2)}) collective-permute-start(bf16[4,464,128]{2,1,0:T(8,128)(2,1)S(1)} %pad_maximum_fusion), channel_id=1, source_target_pairs={{0,32},{1,481},{2,34},{3,483},{4,36},{5,485},{6,38},{7,487},{8,40}... | collective-permute-start | bytes 1425416 | tf_op jit(solution)/shard_map/ppermute | solution.py:34
  177.3 19.7 %collective-permute-start.26 = (bf16[4,464,128]{2,1,0:T(8,128)(2,1)S(1)}, bf16[4,464,128]{2,1,0:T(8,128)(2,1)S(1)}, u32[]{:S(2)}, u32[]{:S(2)}) collective-permute-start(bf16[4,464,128]{2,1,0:T(8,128)(2,1)S(1)} %pad_maximum_fusion.1.refs_0_), channel_id=1, source_target_pairs={{0,32},{1,481},{2,34},{3,483},{4,36},{5,485},{6,38},{7,487},{8,40}... | collective-permute-start | bytes 1425416 | tf_op jit(solution)/shard_map/ppermute | solution.py:34
  180.9 13.9 %collective-permute-start.28 = (bf16[3,464,128]{2,1,0:T(8,128)(2,1)S(1)}, bf16[3,464,128]{2,1,0:T(8,128)(2,1)S(1)}, u32[]{:S(2)}, u32[]{:S(2)}) collective-permute-start(bf16[3,464,128]{2,1,0:T(8,128)(2,1)S(1)} %pad_maximum_fusion.2), channel_id=1, source_target_pairs={{0,1},{1,0},{2,3},{3,2},{4,5},{5,4},{6,7},{7,6},{8,9},{9,8},{10,11... | collective-permute-start | bytes 1069064 | tf_op jit(solution)/shard_map/ppermute | solution.py:38
  187.8 9.2 %collective-permute-start.27 = (bf16[464,128]{1,0:T(8,128)(2,1)S(1)}, bf16[464,128]{1,0:T(8,128)(2,1)S(1)}, u32[]{:S(2)}, u32[]{:S(2)}) collective-permute-start(bf16[464,128]{1,0:T(8,128)(2,1)S(1)} %collective-permute-done.25), channel_id=1, source_target_pairs={{0,64},{1,449},{2,66},{3,451},{4,68},{5,453},{6,70},{7,455},{8,72}... | collective-permute-start | bytes 356360 | tf_op jit(solution)/shard_map/ppermute | solution.py:34
  194.7 1.5 copy-start.23
  197.0 4.7 %copy-start.33 = (bf16[448,384]{1,0:T(8,128)(2,1)}, bf16[448,384]{1,0:T(8,128)(2,1)S(1)}, u32[]{:S(2)}) copy-start(bf16[448,384]{1,0:T(8,128)(2,1)S(1)} %get-tuple-element.119.refs_5_) | copy-start | bytes 1032196
  197.0 4.7 %copy-start.15 = (bf16[16,64,512]{2,1,0:T(8,128)(2,1)}, bf16[16,64,512]{2,1,0:T(8,128)(2,1)S(1)}, u32[]{:S(2)}) copy-start(bf16[16,64,512]{2,1,0:T(8,128)(2,1)S(1)} %collective-permute-done.29.refs_9_) | copy-start | bytes 3145732
  197.1 7.4 %collective-permute-start.30 = (bf16[4,464,128]{2,1,0:T(8,128)(2,1)S(1)}, bf16[4,464,128]{2,1,0:T(8,128)(2,1)S(1)}, u32[]{:S(2)}, u32[]{:S(2)}) collective-permute-start(bf16[4,464,128]{2,1,0:T(8,128)(2,1)S(1)} %collective-permute-done.21), channel_id=1, source_target_pairs={{0,1},{1,0},{2,3},{3,2},{4,5},{5,4},{6,7},{7,6},{8,9},{9,8},{10,11... | collective-permute-start | bytes 1425416 | tf_op jit(solution)/shard_map/ppermute | solution.py:38
  202.5 4.0 %copy-start.27 = (bf16[448,512]{1,0:T(8,128)(2,1)}, bf16[448,512]{1,0:T(8,128)(2,1)S(1)}, u32[]{:S(2)}) copy-start(bf16[448,512]{1,0:T(8,128)(2,1)S(1)} %get-tuple-element.116.refs_2_) | copy-start | bytes 1376260
  202.6 8.0 %collective-permute-start.31 = (bf16[704,512]{1,0:T(8,128)(2,1)S(1)}, bf16[704,512]{1,0:T(8,128)(2,1)S(1)}, u32[]{:S(2)}, u32[]{:S(2)}) collective-permute-start(bf16[704,512]{1,0:T(8,128)(2,1)S(1)} %get-tuple-element.110), channel_id=1, source_target_pairs={{0,1},{1,0},{2,3},{3,2},{4,5},{5,4},{6,7},{7,6},{8,9},{9,8},{10,11... | collective-permute-start | bytes 2162696 | tf_op jit(solution)/shard_map/ppermute | solution.py:38
  208.1 3.7 %collective-permute-start.32 = (bf16[336,512]{1,0:T(8,128)(2,1)S(1)}, bf16[336,512]{1,0:T(8,128)(2,1)S(1)}, u32[]{:S(2)}, u32[]{:S(2)}) collective-permute-start(bf16[336,512]{1,0:T(8,128)(2,1)S(1)} %get-tuple-element.111), channel_id=1, source_target_pairs={{0,1},{1,0},{2,3},{3,2},{4,5},{5,4},{6,7},{7,6},{8,9},{9,8},{10,11... | collective-permute-start | bytes 1032200 | tf_op jit(solution)/shard_map/ppermute | solution.py:38
  213.8 4.8 %copy-start.16 = (bf16[16,64,512]{2,1,0:T(8,128)(2,1)S(1)}, bf16[16,64,512]{2,1,0:T(8,128)(2,1)}, u32[]{:S(2)}) copy-start(bf16[16,64,512]{2,1,0:T(8,128)(2,1)} %copy-done.15) | copy-start | bytes 3145732
  213.8 21.8 %all-to-all-start.2 = ((bf16[16,272,128]{2,1,0:T(8,128)(2,1)}), bf16[16,272,128]{2,1,0:T(8,128)(2,1)S(1)}, u32[]{:S(2)}, u32[]{:S(2)}) async-start(bf16[16,272,128]{2,1,0:T(8,128)(2,1)} %merge_cores.1), calls=%async_computation.2 | async-start | bytes 2228224 | tf_op jit(solution)/shard_map/all_to_all | solution.py:43
  218.6 1.1 copy-start.20
  219.7 1.1 copy-start.22
  220.7 1.0 copy-start.24
  221.7 1.0 copy-start.26
  222.8 1.0 copy-start.28
  223.8 1.0 copy-start.30
  235.6 1.2 copy-start.10
  (8 other events, 6.9 us)
Sparse Core Ops, SparseCore 0:
  10.7 77.7 all-gather.2
